TPU v7x, 512 devices: a whole 4x4x16 slice. The times are simulated.
512 devices in a mesh: dp: 32 (over z, core), seq: 16 (over y, x).
Axes of the slice: x: 4, y: 4, z: 16, core: 2. Of those that a mesh axis runs over, the one named last changes fastest.
Arguments:
- tokens: bfloat16 [32, 64, 64, 1152], P('dp', None, 'seq'), may hold values from -6 to 6
- slot_owner: int32 [32, 64], P('dp'), may hold values from 0 to 31, as said below
- clip_pieces: int32 [32, 4, 16], P('dp'), may hold values from 0 to 63, as said below
- clip_length: int32 [32, 4], P('dp'), may hold values from 256 to 1024, as said below
- modulation: bfloat16 [32, 4, 3, 1152], P('dp'), may hold values from -4 to 4
- qkv_weight: bfloat16 [1152, 3, 1152], P(None, None, 'seq'), may hold values from -0.1875 to 0.1875
- qk_gain: float32 [2, 72], replicated, may hold values from 0.1 to 1.9
- proj_weight: bfloat16 [1152, 1152], P('seq'), may hold values from -0.1875 to 0.1875
Outputs:
- block_output: bfloat16 [32, 64, 64, 1152], P('dp', None, 'seq')
Inputs may be any that keep to these rules, and one draw needn't show every extreme that they name: `slot_owner`: each row names every owner exactly 2 times. `clip_pieces`: each owner's table holds every arrival index 0 to 63 exactly once. `clip_length`: every owner has one clip of 1024 tokens.
All inputs are finite; a program needn't handle non-finite values.
Results may differ from a plain program's by a relative error of at most 0.0045.
Values may be sent and summed in bfloat16 or wider, within the bound.
A program may use at most 64 MiB of HBM per device.

v0:
```python
import math

import jax
import jax.numpy as jnp
from jax import lax
from jax.sharding import PartitionSpec as P

HEADS = 16


EPSILON = 1e-06


def scaled_norm(head_block, gain_row):
    mean_square = jnp.mean(head_block * head_block, axis=-1, keepdims=True)
    return (head_block * lax.rsqrt(mean_square + EPSILON) * gain_row).astype(jnp.bfloat16)


def normalize_heads(projected, qk_gain):
    queries = scaled_norm(projected[..., 0, :, :], qk_gain[0])
    keys_part = scaled_norm(projected[..., 1, :, :], qk_gain[1])
    values = projected[..., 2, :, :].astype(jnp.bfloat16)
    return jnp.stack([queries, keys_part, values], axis=-3)


def attend_clip(operands):
    stacked, length_one = operands
    head_size = stacked.shape[-1]
    scores = jnp.einsum(
        "qhe,khe->hqk", stacked[:, 0], stacked[:, 1], preferred_element_type=jnp.float32
    )
    scores = scores * (1.0 / math.sqrt(head_size))
    positions = jnp.arange(stacked.shape[0], dtype=jnp.int32)
    in_clip = positions < length_one
    unscaled = jnp.where(in_clip[None, None, :], jnp.exp(scores), 0.0)
    weights = (unscaled / jnp.sum(unscaled, axis=-1, keepdims=True)).astype(jnp.bfloat16)
    return jnp.einsum(
        "hqk,khe->qhe", weights, stacked[:, 2], preferred_element_type=jnp.float32
    ).astype(jnp.bfloat16)


def body(
    tokens, slot_owner, clip_pieces, clip_length, modulation, qkv_weight, qk_gain, proj_weight
):
    dp_count = lax.axis_size("dp")
    seq_count = lax.axis_size("seq")
    pieces_here = tokens.shape[1]
    piece_rows = tokens.shape[2]
    model_width = tokens.shape[3]
    per_peer = pieces_here // dp_count
    head_size = qk_gain.shape[1]
    local_heads = HEADS // seq_count
    sorted_slots = jnp.argsort(slot_owner[0], stable=True)
    outgoing = tokens[0][sorted_slots].reshape(dp_count, per_peer, piece_rows, model_width)
    arrived = lax.all_to_all(outgoing, "dp", split_axis=0, concat_axis=0, tiled=True).reshape(
        pieces_here, piece_rows, model_width
    )
    piece_table = clip_pieces[0]
    clips_here = piece_table.shape[0]
    per_clip = piece_table.shape[1]
    clip_rows = arrived[piece_table.reshape(-1)].reshape(
        clips_here, per_clip, piece_rows, model_width
    )
    factors = modulation[0].astype(jnp.float32)
    clip_float = clip_rows.astype(jnp.float32)
    average = jnp.mean(clip_float, axis=-1, keepdims=True)
    centered = clip_float - average
    variance = jnp.mean(centered * centered, axis=-1, keepdims=True)
    normed = centered * lax.rsqrt(variance + EPSILON)
    hidden = (
        normed * (1.0 + factors[:, 1][:, None, None, :]) + factors[:, 0][:, None, None, :]
    ).astype(jnp.bfloat16)
    flat_hidden = hidden.reshape(-1, model_width)
    projected = jnp.einsum(
        "nd,dtc->ntc",
        flat_hidden,
        lax.all_gather(qkv_weight, "seq", axis=2, tiled=True),
        preferred_element_type=jnp.float32,
    )
    projected = projected.reshape(clips_here, per_clip, piece_rows, 3, HEADS, head_size)
    local_triple = normalize_heads(projected, qk_gain)
    grouped = lax.all_to_all(local_triple, "seq", split_axis=4, concat_axis=2, tiled=True)
    clip_tokens = per_clip * piece_rows * seq_count
    sequences = grouped.reshape(clips_here, clip_tokens, 3, local_heads, head_size)
    attended = lax.map(attend_clip, (sequences, clip_length[0]))
    attended = attended.reshape(
        clips_here, per_clip, piece_rows * seq_count, local_heads, head_size
    )
    returned_heads = lax.all_to_all(attended, "seq", split_axis=2, concat_axis=3, tiled=True)
    flat_heads = returned_heads.reshape(-1, HEADS * head_size)
    branch = jnp.dot(
        flat_heads,
        lax.all_gather(proj_weight, "seq", axis=0, tiled=True),
        preferred_element_type=jnp.float32,
    )
    branch = branch.reshape(clips_here, per_clip, piece_rows, model_width)
    positions = (
        jnp.arange(per_clip, dtype=jnp.int32)[:, None] * (piece_rows * seq_count)
        + lax.axis_index("seq") * piece_rows
        + jnp.arange(piece_rows, dtype=jnp.int32)[None, :]
    )
    in_clip = positions[None] < clip_length[0][:, None, None]
    result = jnp.where(
        in_clip[..., None], clip_float + factors[:, 2][:, None, None, :] * branch, 0.0
    ).astype(jnp.bfloat16)
    inverse = jnp.argsort(piece_table.reshape(-1))
    home_pieces = result.reshape(pieces_here, piece_rows, model_width)[inverse]
    home_pieces = home_pieces.reshape(dp_count, per_peer, piece_rows, model_width)
    came_back = lax.all_to_all(home_pieces, "dp", split_axis=0, concat_axis=0, tiled=True).reshape(
        pieces_here, piece_rows, model_width
    )
    slot_ranks = jnp.argsort(sorted_slots)
    return came_back[slot_ranks][None]


def solution(mesh):
    return jax.shard_map(
        body,
        mesh=mesh,
        in_specs=(
            P("dp", None, "seq", None),
            P("dp", None),
            P("dp", None, None),
            P("dp", None),
            P("dp", None, None, None),
            P(None, None, "seq"),
            P(),
            P("seq", None),
        ),
        out_specs=P("dp", None, "seq", None),
        check_vma=False,
    )
```

profile of v0, /device:TPU:1, one launch (start us, length us, event | category | flops | bytes accessed | tf_op | source)
XLA Modules:
  0.0 279.0 jit_solution(16358597132218547745)
XLA Ops:
  6.5 0.0 copy-start
  6.5 0.0 all-gather.3.cloned.1.call-start
  6.6 0.7 all-gather.3.cloned.1.call-update
  7.3 2.7 sort.48
  10.0 1.9 gather_fusion
  11.8 16.8 %all-to-all-start = ((bf16[32,2,4,1152]{3,2,1,0:T(4,128)(2,1)}), bf16[32,2,4,1152]{3,2,1,0:T(4,128)(2,1)S(1)}, u32[]{:S(2)}, u32[]{:S(2)}) async-start(bf16[32,2,4,1152]{3,2,1,0:T(4,128)(2,1)} %bitcast.11), calls=%async_computation | async-start | bytes 1179648 | tf_op jit(solution)/shard_map/all_to_all | solution.py:55
  28.6 0.0 copy-done.3
  28.6 0.1 reshape_squeeze.6
  28.8 0.6 slice_bitcast_fusion.7
  29.4 35.5 %all-to-all-done = bf16[32,2,4,1152]{3,2,1,0:T(4,128)(2,1)S(1)} async-done(((bf16[32,2,4,1152]{3,2,1,0:T(4,128)(2,1)}), bf16[32,2,4,1152]{3,2,1,0:T(4,128)(2,1)S(1)}, u32[]{:S(2)}, u32[]{:S(2)}) %all-to-all-start) | async-done | bytes 589856 | tf_op jit(solution)/shard_map/all_to_all | solution.py:55
  64.9 1.1 gather_fusion.1
  66.0 0.3 convert_reduce_fusion
  66.3 0.5 multiply_reduce_fusion.2
  66.9 0.6 add_convert_fusion
  67.5 32.6 %all-gather.3.cloned.1.call-done = bf16[1152,3,1152]{0,2,1:T(8,128)(2,1)} async-done(((bf16[1152,3,72]{0,2,1:T(8,128)(2,1)}), bf16[1152,3,1152]{0,2,1:T(8,128)(2,1)}) %all-gather.3.cloned.1.call-update) | async-done | bytes 7962640 | tf_op jit(solution)/shard_map/all_gather | solution.py:77
  100.1 6.6 %fusion.14 = f32[4,16,4,3,16,72]{5,1,4,3,2,0:T(8,128)S(1)} fusion(bf16[3,16,72,1152,1,1]{3,2,1,0,5,4:T(8,128)(2,1)} %bitcast.109, bf16[4,16,4,1152,1,1]{3,2,1,0,5,4:T(4,128)(2,1)S(1)} %bitcast.107), kind=kOutput, calls=%fused_computation.33 | convolution fusion | flops 2038431744 | bytes 12091392 | tf_op jit(solution)/shard_map/nd,dtc->ntc/dot_general | solution.py:74
  106.7 1.2 multiply_reduce_fusion.1
  107.8 0.2 slice.77
  108.0 1.3 multiply_convert_fusion.1
  109.4 0.7 pad_maximum_fusion
  110.1 2.6 copy.29
  112.7 5.0 %all-to-all-start.1 = ((bf16[4,16,4,3,16,72]{5,1,3,2,0,4:T(8,128)(2,1)}), bf16[4,16,4,3,16,72]{5,1,3,2,0,4:T(8,128)(2,1)}, u32[]{:S(2)}, u32[]{:S(2)}) async-start(bf16[4,16,4,3,16,72]{5,1,3,2,0,4:T(8,128)(2,1)} %copy.29), calls=%async_computation.1 | async-start | bytes 6291456 | tf_op jit(solution)/shard_map/all_to_all | solution.py:82
  117.7 0.2 all-gather.5.cloned.1.call-start
  117.9 0.5 all-gather.5.cloned.1.call-update
  118.5 0.1 reshape_squeeze.7
  118.6 2.1 sort.49
  120.6 44.7 %all-to-all-done.1 = bf16[4,16,4,3,16,72]{5,1,3,2,0,4:T(8,128)(2,1)} async-done(((bf16[4,16,4,3,16,72]{5,1,3,2,0,4:T(8,128)(2,1)}), bf16[4,16,4,3,16,72]{5,1,3,2,0,4:T(8,128)(2,1)}, u32[]{:S(2)}, u32[]{:S(2)}) %all-to-all-start.1) | async-done | bytes 1769504 | tf_op jit(solution)/shard_map/all_to_all | solution.py:82
  165.3 5.3 %copy.30 = bf16[4,16,16,4,3,1,72]{6,3,2,1,4,0,5:T(4,128)(2,1)} copy(bf16[4,16,16,4,3,1,72]{6,1,4,3,0,2,5:T(8,128)(2,1)} %bitcast.31) | data formatting | bytes 3538944 | tf_op jit(solution)/shard_map/all_to_all | solution.py:82
  170.7 3.1 %copy.31 = bf16[4,1024,3,1,72]{1,4,3,2,0:T(8,128)(2,1)S(1)} copy(bf16[4,1024,3,1,72]{4,1,2,0,3:T(8,128)(2,1)} %bitcast.100) | data formatting | bytes 3538944 | tf_op jit(solution)/shard_map/while | solution.py:85
  173.8 13.9 %while.10 = (s32[]{:T(128)}, bf16[4,1024,1,72]{1,3,2,0:T(8,128)(2,1)S(1)}, bf16[4,1024,3,1,72]{1,4,3,2,0:T(8,128)(2,1)S(1)}, s32[4]{0:T(128)S(1)}, s32[]{:T(128)}) while((s32[]{:T(128)}, bf16[4,1024,1,72]{1,3,2,0:T(8,128)(2,1)S(1)}, bf16[4,1024,3,1,72]{1,4,3,2,0:T(8,128)(2,1)S(1)}, s32[4]{0:T(128)S(1)}, s32[]{:T(128)}) %tuple.37), condition=%wide.region_7.8_spmd, body=%wide.region_5.7_spmd.sunk | while | flops 309403648 | bytes 9874517 | solution.py:85
  173.9 0.7 dynamic_slice.12
  174.5 0.7 iota_compare_fusion.2
  175.2 1.0 fusion.22
  176.3 1.0 fusion.23
  177.3 0.7 dynamic_slice.12
  178.0 0.7 iota_compare_fusion.2
  178.7 1.0 fusion.22
  179.7 1.0 fusion.23
  180.8 0.7 dynamic_slice.12
  181.5 0.7 iota_compare_fusion.2
  182.2 1.0 fusion.22
  183.2 1.0 fusion.23
  184.3 0.7 dynamic_slice.12
  185.0 0.7 iota_compare_fusion.2
  185.7 1.0 fusion.22
  186.7 1.0 fusion.23
  187.7 0.7 reshape.247
  188.4 2.8 %copy.32 = bf16[4,16,64,1,72]{4,1,3,0,2:T(8,128)(2,1)} copy(bf16[4,16,64,1,72]{2,1,4,0,3:T(8,128)(2,1)S(1)} %reshape.247) | data formatting | bytes 1179648 | tf_op jit(solution)/shard_map/reshape | solution.py:86
  191.3 4.6 %all-to-all-start.2 = ((bf16[4,16,64,1,72]{4,1,3,0,2:T(8,128)(2,1)}), bf16[4,16,64,1,72]{4,1,3,0,2:T(8,128)(2,1)S(1)}, u32[]{:S(2)}, u32[]{:S(2)}) async-start(bf16[4,16,64,1,72]{4,1,3,0,2:T(8,128)(2,1)} %copy.32), calls=%async_computation.2 | async-start | bytes 2097152 | tf_op jit(solution)/shard_map/all_to_all | solution.py:89
  195.9 0.1 broadcast_compare_fusion
  196.0 0.1 convert.13
  196.1 14.8 %all-to-all-done.2 = bf16[4,16,64,1,72]{4,1,3,0,2:T(8,128)(2,1)S(1)} async-done(((bf16[4,16,64,1,72]{4,1,3,0,2:T(8,128)(2,1)}), bf16[4,16,64,1,72]{4,1,3,0,2:T(8,128)(2,1)S(1)}, u32[]{:S(2)}, u32[]{:S(2)}) %all-to-all-start.2) | async-done | bytes 589856 | tf_op jit(solution)/shard_map/all_to_all | solution.py:89
  210.8 0.2 copy.33
  211.0 0.7 copy.34
  211.7 1.3 dot_general.21
  213.0 0.0 all-gather.5.cloned.1.call-done
  213.0 0.0 copy-done.2
  213.0 2.8 fusion.11
  215.8 0.5 copy.37
  216.3 1.9 gather_fusion.2
  218.2 15.9 %all-to-all-start.3 = ((bf16[32,2,4,1152]{3,2,1,0:T(4,128)(2,1)}), bf16[32,2,4,1152]{3,2,1,0:T(4,128)(2,1)S(1)}, u32[]{:S(2)}, u32[]{:S(2)}) async-start(bf16[32,2,4,1152]{3,2,1,0:T(4,128)(2,1)} %bitcast.38), calls=%async_computation.3 | async-start | bytes 1179648 | tf_op jit(solution)/shard_map/all_to_all | solution.py:109
  234.1 2.1 sort.50
  236.2 34.1 %all-to-all-done.3 = bf16[32,2,4,1152]{3,2,1,0:T(4,128)(2,1)S(1)} async-done(((bf16[32,2,4,1152]{3,2,1,0:T(4,128)(2,1)}), bf16[32,2,4,1152]{3,2,1,0:T(4,128)(2,1)S(1)}, u32[]{:S(2)}, u32[]{:S(2)}) %all-to-all-start.3) | async-done | bytes 589856 | tf_op jit(solution)/shard_map/all_to_all | solution.py:109
  270.4 1.9 gather_fusion.3
  (35 shorter events, 0.4 us)
Async XLA Ops:
  6.5 3.4 %copy-start = (bf16[1,64,4,1152]{3,2,1,0:T(4,128)(2,1)S(1)}, bf16[1,64,4,1152]{3,2,1,0:T(4,128)(2,1)}, u32[]{:S(2)}) copy-start(bf16[1,64,4,1152]{3,2,1,0:T(4,128)(2,1)} %param.10) | copy-start | bytes 1769476
  6.5 22.1 %copy-start.3 = (s32[1,4,16]{2,1,0:T(4,128)S(1)}, s32[1,4,16]{2,1,0:T(4,128)}, u32[]{:S(2)}) copy-start(s32[1,4,16]{2,1,0:T(4,128)} %param.12) | copy-start | bytes 772
  6.5 22.2 %copy-start.4 = (f32[2,72]{1,0:T(2,128)S(1)}, f32[2,72]{1,0:T(2,128)}, u32[]{:S(2)}) copy-start(f32[2,72]{1,0:T(2,128)} %param.16) | copy-start | bytes 1732
  6.5 22.2 %copy-start.1 = (bf16[1,4,3,1152]{3,1,2,0:T(4,128)(2,1)S(1)}, bf16[1,4,3,1152]{3,1,2,0:T(4,128)(2,1)}, u32[]{:S(2)}) copy-start(bf16[1,4,3,1152]{3,1,2,0:T(4,128)(2,1)} %param.14) | copy-start | bytes 82948
  6.5 93.5 %all-gather.3.cloned.1.call-start = ((), (), s32[]{:S(2)}) async-start(), calls=%async_computation.4 | async-start | bytes 8460288 | tf_op jit(solution)/shard_map/all_gather | solution.py:77
  11.8 53.0 %all-to-all-start = ((bf16[32,2,4,1152]{3,2,1,0:T(4,128)(2,1)}), bf16[32,2,4,1152]{3,2,1,0:T(4,128)(2,1)S(1)}, u32[]{:S(2)}, u32[]{:S(2)}) async-start(bf16[32,2,4,1152]{3,2,1,0:T(4,128)(2,1)} %bitcast.11), calls=%async_computation | async-start | bytes 1179648 | tf_op jit(solution)/shard_map/all_to_all | solution.py:55
  112.7 52.6 %all-to-all-start.1 = ((bf16[4,16,4,3,16,72]{5,1,3,2,0,4:T(8,128)(2,1)}), bf16[4,16,4,3,16,72]{5,1,3,2,0,4:T(8,128)(2,1)}, u32[]{:S(2)}, u32[]{:S(2)}) async-start(bf16[4,16,4,3,16,72]{5,1,3,2,0,4:T(8,128)(2,1)} %copy.29), calls=%async_computation.1 | async-start | bytes 6291456 | tf_op jit(solution)/shard_map/all_to_all | solution.py:82
  117.7 95.3 %all-gather.5.cloned.1.call-start = ((), (), s32[]{:S(2)}) async-start(), calls=%async_computation.5 | async-start | bytes 2820096 | tf_op jit(solution)/shard_map/all_gather | solution.py:93
  170.7 3.2 %copy-start.5 = (s32[1,4]{1,0:T(1,128)S(1)}, s32[1,4]{1,0:T(1,128)}, u32[]{:S(2)}) copy-start(s32[1,4]{1,0:T(1,128)} %param.13) | copy-start | bytes 52
  191.3 19.5 %all-to-all-start.2 = ((bf16[4,16,64,1,72]{4,1,3,0,2:T(8,128)(2,1)}), bf16[4,16,64,1,72]{4,1,3,0,2:T(8,128)(2,1)S(1)}, u32[]{:S(2)}, u32[]{:S(2)}) async-start(bf16[4,16,64,1,72]{4,1,3,0,2:T(8,128)(2,1)} %copy.32), calls=%async_computation.2 | async-start | bytes 2097152 | tf_op jit(solution)/shard_map/all_to_all | solution.py:89
  211.0 2.0 copy-start.2
  218.2 52.2 %all-to-all-start.3 = ((bf16[32,2,4,1152]{3,2,1,0:T(4,128)(2,1)}), bf16[32,2,4,1152]{3,2,1,0:T(4,128)(2,1)S(1)}, u32[]{:S(2)}, u32[]{:S(2)}) async-start(bf16[32,2,4,1152]{3,2,1,0:T(4,128)(2,1)} %bitcast.38), calls=%async_computation.3 | async-start | bytes 1179648 | tf_op jit(solution)/shard_map/all_to_all | solution.py:109
Sparse Core Ops, SparseCore 0:
  10.4 89.5 all-gather.2
  121.6 77.9 all-gather.4
where the time goes:
time: 280 us; the launch traced here: 279 us
  waiting for transfers between devices  163 us (58%)
  starting transfers between devices  42.5 us (15%)
  local copies, waits for them, and re-layouts  27.2 us (10%)
  matrix products  17.5 us (6%)
  other arithmetic  15.1 us (5%)
  between operations  13.7 us (5%)
    all_to_all x1, waiting for transfers between devices, body(): lax.all_to_all(local_triple, 'seq', split_axis=4, concat_axis=2, tiled=True)  44.7 us
    all_to_all x1, waiting for transfers between devices, body(): lax.all_to_all(outgoing, 'dp', split_axis=0, concat_axis=0, tiled=True)  35.5 us
    all_to_all x1, waiting for transfers between devices, body(): lax.all_to_all(home_pieces, 'dp', split_axis=0, concat_axis=0, tiled=True)  34.1 us
    all_gather x1, waiting for transfers between devices, body(): lax.all_gather(qkv_weight, 'seq', axis=2, tiled=True)  32.6 us
    all_to_all x1, starting transfers between devices, body(): lax.all_to_all(outgoing, 'dp', split_axis=0, concat_axis=0, tiled=True)  16.8 us
    all_to_all x1, starting transfers between devices, body(): lax.all_to_all(home_pieces, 'dp', split_axis=0, concat_axis=0, tiled=True)  15.9 us
    all_to_all x1, waiting for transfers between devices, body(): lax.all_to_all(attended, 'seq', split_axis=2, concat_axis=3, tiled=True)  14.8 us
    dot_general x1, matrix products, body(): jnp.einsum('nd,dtc->ntc', flat_hidden, lax.all_gather(qkv_weight, 'seq',...  6.58 us
  transfers between devices with their start and end apart: 6, of which 5 were waited for; matrix products, arithmetic and copies ran while one was open for 14% of the time, Pallas kernels for 0%

commit v1 on v0

v1 whole, which is shorter than its diff:
```python
import math

import jax
import jax.numpy as jnp
from jax import lax
from jax.experimental import pallas as pl
from jax.experimental.pallas import tpu as pltpu
from jax.sharding import PartitionSpec as P

MESH = pl.DeviceIdType.MESH
F32 = jnp.float32
BF16 = jnp.bfloat16
I32 = jnp.int32
D = 1152
HD = 72
N_DP = 32
N_SEQ = 16
NX = 4
NY = 4
CLIPS = 4
HALF = 640
REST = D - HALF
CHUNKS = 4
PER_CHUNK = N_DP // CHUNKS
ROWS = 256
CHUNK_ROWS = ROWS // CHUNKS
EPSILON = 1e-06


def iota(shape, dim):
    return lax.broadcasted_iota(I32, shape, dim)


def mm(a, b):
    return lax.dot_general(a, b, (((1,), (0,)), ((), ())), preferred_element_type=F32)


def mm_nt(a, b):
    return lax.dot_general(a, b, (((1,), (1,)), ((), ())), preferred_element_type=F32)


def slot_of(distance):
    return jnp.where(distance < 16, 2 * (16 - distance) - 1, 2 * (distance - 16))


def distance_of(slot):
    k = (slot + 1) // 2
    return 16 + k * (1 - 2 * (slot % 2))


def column_of(row, n):
    spread = jnp.broadcast_to(row.astype(F32), (n, n))
    picked = jnp.where(iota((n, n), 0) == iota((n, n), 1), spread, 0.0)
    return jnp.sum(picked, axis=1, keepdims=True).astype(I32)


def kernel(
    tok, owner, table, length, mod, w, gain, pw, out,
    outgoing, arrived, hid, wall, wcat, res, pwall, pwcat, stage, qkv, qc, kc, vc, att, attsend, attin,
    ret, back, spread, spread_t, unroute, route, clip_col,
    dp_send, dp_recv, y_send, y_recv, x_send, x_recv, w_send, w_recv, wf_send, wf_recv,
    p_send, p_recv, pf_send, pf_recv, a_send, a_recv, r_send, r_recv, local, x_local,
):
    me = lax.axis_index("dp")
    sq = lax.axis_index("seq")
    core = me % 2
    sibling = me + 1 - 2 * core
    y = sq // NX
    x = sq % NX

    def remote(src, dst, send, recv, dp, seq):
        return pltpu.make_async_remote_copy(
            src_ref=src, dst_ref=dst, send_sem=send, recv_sem=recv,
            device_id={"dp": dp, "seq": seq}, device_id_type=MESH,
        )

    def tok_out(i):
        return remote(outgoing.at[i], arrived.at[i], dp_send.at[i], dp_recv.at[i], (me + distance_of(i)) % N_DP, sq)

    def ret_out(i):
        return remote(
            ret.at[i], back.at[i], r_send.at[i], r_recv.at[i], (me - distance_of(i) + N_DP) % N_DP, sq
        )

    def hid_copy(k, step, row):
        return remote(
            hid.at[k, row], hid.at[k, row], y_send.at[k, step], y_recv.at[k, step], me, ((y + step) % NY) * NX + x
        )

    def w_copy(step, col):
        return remote(
            wall.at[col, core], wall.at[col, core], w_send.at[step], w_recv.at[step], me, y * NX + (x + step) % NX
        )

    def w_forward(step, half):
        col = (x - step + NX) % NX
        return remote(wall.at[col, half], wall.at[col, half], wf_send.at[step], wf_recv.at[step], sibling, sq)

    def x_copy(k, step, col):
        return remote(
            stage.at[k, (x + step) % NX], qkv.at[col, k], x_send.at[k, step], x_recv.at[k, step],
            me, y * NX + (x + step) % NX,
        )

    def p_copy(step, head):
        return remote(
            pwall.at[core, head], pwall.at[core, head], p_send.at[step], p_recv.at[step], me, (sq + step) % N_SEQ
        )

    def p_forward(step, half):
        head = (sq - step + N_SEQ) % N_SEQ
        return remote(pwall.at[half, head], pwall.at[half, head], pf_send.at[step], pf_recv.at[step], sibling, sq)

    def a_copy(step, head):
        to = (sq + step) % N_SEQ
        return remote(attsend.at[to], attin.at[head], a_send.at[step], a_recv.at[step], me, to)

    def each(first, last, action):
        lax.fori_loop(first, last, lambda i, c: (action(i), c)[1], 0)

    barrier = pltpu.get_barrier_semaphore()
    each(1, N_DP, lambda i: pl.semaphore_signal(
        barrier, inc=1, device_id={"dp": (me + i) % N_DP, "seq": sq}, device_id_type=MESH))
    each(1, N_SEQ, lambda i: pl.semaphore_signal(
        barrier, inc=1, device_id={"dp": me, "seq": (sq + i) % N_SEQ}, device_id_type=MESH))

    own = []
    for half in range(2):
        cols = pl.ds(half * REST, HALF)
        own.append(pltpu.make_async_copy(w.at[:, :, cols], wall.at[x, half], local.at[half]))
        own.append(pltpu.make_async_copy(pw.at[:, cols], pwall.at[half, sq], local.at[2 + half]))
    for copy in own:
        copy.start()

    owners = owner[...]
    owners_f = jnp.broadcast_to(owners.astype(F32), (64, 64))
    owners_col = column_of(owners, 64).astype(F32)
    earlier = (owners_col == owners_f) & (iota((64, 64), 0) < iota((64, 64), 1))
    rank = jnp.sum(jnp.where(earlier, 1.0, 0.0), axis=0, keepdims=True).astype(I32)
    piece_key = slot_of((owners - me + N_DP) & (N_DP - 1)) * 8 + rank * 4
    widen = jnp.where((iota((64, ROWS), 1) >> 2) == iota((64, ROWS), 0), 1.0, 0.0).astype(BF16)
    keys = mm(jnp.broadcast_to(piece_key.astype(F32), (16, 64)).astype(BF16), widen)[0:1].astype(I32)
    keys = keys + (iota((1, ROWS), 1) & 3)
    route_rows = jnp.where(iota((ROWS, ROWS), 0) == keys, 1.0, 0.0).astype(BF16)
    outgoing[...] = mm(route_rows, tok[...]).reshape(N_DP, 8, D).astype(BF16)

    pl.semaphore_wait(barrier, N_DP - 1 + N_SEQ - 1)

    own[0].wait()
    own[2].wait()
    for step in (2, 1, 3):
        w_copy(step, x).start()
    each(0, N_DP - 1, lambda i: tok_out(i).start())
    self_in = pltpu.make_async_copy(outgoing.at[N_DP - 1], arrived.at[N_DP - 1], local.at[4])
    self_in.start()

    keys_col = column_of(keys, ROWS)
    route[...] = jnp.where(iota((ROWS, ROWS), 1) == keys_col, 1.0, 0.0).astype(BF16)

    def arrival_row(pieces, row):
        source, rank_of = pieces >> 1, pieces & 1
        return slot_of((me - source + N_DP) & (N_DP - 1)) * 8 + rank_of * 4 + row

    def table_row(width, clip_shift):
        lane = iota((16, width), 1)
        pick = jnp.where(((lane >> 2) & 15) == iota((16, width), 0), 1.0, 0.0).astype(BF16)
        wide = mm(table[...].astype(F32).astype(BF16), pick)
        mine = (iota((CLIPS, width), 1) >> clip_shift) == iota((CLIPS, width), 0)
        pieces = jnp.sum(jnp.where(mine, wide, 0.0), axis=0, keepdims=True).astype(I32)
        return arrival_row(pieces, iota((1, width), 1) & 3)

    key_short = table_row(ROWS, 6)
    of_clip = iota((ROWS, ROWS), 0) == key_short
    unroute[...] = jnp.where(of_clip, 1.0, 0.0).astype(BF16)
    place = jnp.sum(jnp.where(of_clip, iota((ROWS, ROWS), 1).astype(F32), 0.0), axis=1, keepdims=True)
    clip_col[...] = jnp.broadcast_to(place.astype(I32), (ROWS, 128))
    key_long = table_row(2 * ROWS, 7)
    wide_lane = iota((1, 2 * ROWS), 1)
    key_long = (key_long >> 6) * 128 + ((wide_lane >> 6) & 1) * 64 + (key_long & 63)
    spread[...] = jnp.where(iota((512, 512), 0) == key_long, 1.0, 0.0).astype(BF16)
    spread_t[...] = jnp.where(iota((512, 512), 1) == column_of(key_long, 512), 1.0, 0.0).astype(BF16)

    def of_its_clip(clip, which):
        factors = mod[which].astype(F32)
        rows = [factors[c:c + 1, :] for c in range(CLIPS)]
        return jnp.where(clip == 0, rows[0], jnp.where(clip == 1, rows[1], jnp.where(clip == 2, rows[2], rows[3])))

    def chunk_in(k, last):
        def wait(i):
            tok_out(i).wait_recv()
        each(k * PER_CHUNK, (k + 1) * PER_CHUNK - (1 if last else 0), wait)
        if last:
            self_in.wait()
        rows = arrived[pl.ds(k * PER_CHUNK, PER_CHUNK)].astype(F32).reshape(CHUNK_ROWS, D)
        clip = clip_col[pl.ds(pl.multiple_of(k * CHUNK_ROWS, CHUNK_ROWS), CHUNK_ROWS), 0:1] >> 6
        centered = rows - jnp.mean(rows, axis=-1, keepdims=True)
        variance = jnp.mean(centered * centered, axis=-1, keepdims=True)
        normed = centered * lax.rsqrt(variance + EPSILON)
        hidden = normed * (1.0 + of_its_clip(clip, 1)) + of_its_clip(clip, 0)
        hid[k, pl.ds(y, 1)] = hidden.astype(BF16)[None]
        for step in (2, 1, 3):
            hid_copy(k, step, y).start()

    gains = []
    for i in range(2):
        spread_gain = jnp.broadcast_to(gain[i:i + 1, :], (HD, HD))
        picked = jnp.where(iota((HD, HD), 0) == iota((HD, HD), 1), spread_gain, 0.0)
        gains.append(jnp.sum(picked, axis=1, keepdims=True))

    def own_stage(k):
        return pltpu.make_async_copy(stage.at[k, x], qkv.at[x, k], x_local.at[k])

    def chunk_qkv(k):
        for step in (1, 2, 3):
            hid_copy(k, step, (y - step + NY) % NY).wait_recv()
        rows = hid[k].reshape(ROWS, D)
        res[...] = mm_nt(wcat[...], rows)
        for head in range(NX):
            base = head * 3 * HD
            for part in range(2):
                block = res[base + part * HD:base + (part + 1) * HD, :]
                mean_square = jnp.mean(block * block, axis=0, keepdims=True)
                stage[k, head, part] = (block * lax.rsqrt(mean_square + EPSILON) * gains[part]).astype(BF16)
            stage[k, head, 2] = res[base + 2 * HD:base + 3 * HD, :].astype(BF16)
        for step in (2, 1, 3):
            x_copy(k, step, x).start()
        own_stage(k).start()

    chunk_in(0, False)
    for step in (1, 2, 3):
        w_copy(step, (x - step + NX) % NX).wait_recv()
        w_forward(step, core).start()
    chunk_in(1, False)
    for step in (1, 2, 3):
        w_forward(step, 1 - core).wait_recv()
    for pair in range(NX // 2):
        rows = slice(pair * 6 * HD, (pair + 1) * 6 * HD)
        cols = slice(2 * pair, 2 * pair + 2)
        wcat[rows, 0:HALF] = wall[cols, 0].astype(F32).reshape(6 * HD, HALF).astype(BF16)
        wcat[rows, HALF:D] = wall[cols, 1].astype(F32).reshape(6 * HD, HALF)[:, HALF - REST:].astype(BF16)
    chunk_qkv(0)
    chunk_in(2, False)
    chunk_qkv(1)
    chunk_in(3, True)
    chunk_qkv(2)
    chunk_qkv(3)

    own[1].wait()
    own[3].wait()
    each(1, N_SEQ, lambda i: p_copy(i, sq).start())

    for k in range(CHUNKS):
        own_stage(k).wait()
        for step in (1, 2, 3):
            x_copy(k, step, (x - step + NX) % NX).wait_recv()
    lane = iota((1, 128), 1)

    def to_clips(col, carry):
        for pair in range(2):
            def part_of(part):
                blocks = [qkv[col, k, part, :, pair * 128:(pair + 1) * 128] for k in range(CHUNKS)]
                return jnp.concatenate(blocks, axis=1)
            queries = mm(part_of(0), spread[...]).astype(BF16)
            keys_of = mm_nt(spread_t[...], part_of(1)).astype(BF16)
            values = mm(part_of(2), spread[...])
            for clip in range(CLIPS):
                cut = slice(clip * 128, (clip + 1) * 128)
                qc[clip, col * 2 + pair] = queries[:, cut]
                kc[clip, col * 2 + pair] = keys_of[cut, :]
                position = ((lane >> 2) & 15) * 64 + ((pair * 2 + (lane >> 6)) * NX + col) * 4 + (lane & 3)
                inside = jnp.where(position < length[0, clip], 1.0, 0.0)
                ones = jnp.broadcast_to(inside, (8, 128))
                vc[clip, col * 2 + pair] = jnp.concatenate([values[:, cut] * inside, ones], axis=0).astype(BF16)
        return carry

    lax.fori_loop(0, NX, to_clips, 0)

    factor = math.log2(math.e) / math.sqrt(HD)

    def attend(clip, carry):
        keys_of = kc[clip].reshape(8 * 128, HD)
        values = jnp.concatenate([vc[clip, j] for j in range(8)], axis=1)
        for block in range(4):
            queries = jnp.concatenate([qc[clip, 2 * block], qc[clip, 2 * block + 1]], axis=1)
            scores = mm(keys_of, queries)
            unscaled = jnp.exp2(scores * factor).astype(BF16)
            summed = mm(values, unscaled)
            attended = (summed[0:HD] / summed[HD:HD + 1]).astype(BF16)
            att[clip, 2 * block] = attended[:, 0:128]
            att[clip, 2 * block + 1] = attended[:, 128:256]
        return carry

    lax.fori_loop(0, 2, attend, 0)
    each(1, N_SEQ, lambda i: p_copy(i, (sq - i + N_SEQ) % N_SEQ).wait_recv())
    each(1, N_SEQ, lambda i: p_forward(i, core).start())
    lax.fori_loop(2, CLIPS, attend, 0)

    come = iota((512, 512), 0)
    go = iota((512, 512), 1)
    swap = jnp.where(come == ((go >> 6) & 3) * 128 + (go >> 8) * 64 + (go & 63), 1.0, 0.0).astype(BF16)
    for pair in range(8):
        blocks = jnp.concatenate([att[clip, pair] for clip in range(CLIPS)], axis=1)
        swapped = mm(blocks, swap).astype(BF16)
        for half in range(2):
            attsend[((pair % 2) * 2 + half) * NX + pair // 2] = swapped[:, half * ROWS:(half + 1) * ROWS]
    each(1, N_SEQ, lambda i: a_copy(i, sq).start())
    self_att = pltpu.make_async_copy(attsend.at[sq], attin.at[sq], local.at[5])
    self_att.start()

    each(1, N_SEQ, lambda i: p_forward(i, 1 - core).wait_recv())
    for head in range(N_SEQ // 2):
        rows = pl.ds(head * 2 * HD, 2 * HD)
        pwcat[rows, 0:HALF] = pwall[0, 2 * head:2 * head + 2].astype(F32).reshape(2 * HD, HALF).astype(BF16)
        pwcat[rows, HALF:D] = (
            pwall[1, 2 * head:2 * head + 2].astype(F32).reshape(2 * HD, HALF)[:, HALF - REST:].astype(BF16))

    self_att.wait()
    each(1, N_SEQ, lambda i: a_copy(i, (sq - i + N_SEQ) % N_SEQ).wait_recv())
    heads = attin[...].astype(F32).reshape(N_SEQ * HD, ROWS).astype(BF16)
    for part in range(2):
        half_rows = ROWS // 2
        cut = slice(part * half_rows, (part + 1) * half_rows)
        joined = mm_nt(unroute[cut, :], heads).astype(BF16)
        branch = mm(joined, pwcat[...])
        where = clip_col[cut, 0:1]
        clip = where >> 6
        position = ((where >> 2) & 15) * 64 + sq * 4 + (where & 3)
        limit = jnp.where(clip == 0, length[0, 0], jnp.where(
            clip == 1, length[0, 1], jnp.where(clip == 2, length[0, 2], length[0, 3])))
        rows = arrived[part * 16:(part + 1) * 16].astype(F32).reshape(half_rows, D)
        result = jnp.where(position < limit, rows + of_its_clip(clip, 2) * branch, 0.0)
        ret[part * 16:(part + 1) * 16] = result.reshape(16, 8, D).astype(BF16)
        each(part * 16, part * 16 + 16 - part, lambda i: ret_out(i).start())
    self_back = pltpu.make_async_copy(ret.at[N_DP - 1], back.at[N_DP - 1], local.at[6])
    self_back.start()

    for step in (1, 2, 3):
        w_copy(step, x).wait_send()
        w_forward(step, core).wait_send()
        for k in range(CHUNKS):
            hid_copy(k, step, y).wait_send()
            x_copy(k, step, x).wait_send()
    each(0, N_DP - 1, lambda i: tok_out(i).wait_send())
    each(1, N_SEQ, lambda i: p_copy(i, sq).wait_send())
    each(1, N_SEQ, lambda i: p_forward(i, core).wait_send())
    each(1, N_SEQ, lambda i: a_copy(i, sq).wait_send())

    self_back.wait()
    each(0, N_DP - 1, lambda i: ret_out(i).wait_recv())
    returned = back[...].astype(F32).reshape(ROWS, D).astype(BF16)
    out[...] = mm(route[...], returned).astype(BF16)
    each(0, N_DP - 1, lambda i: ret_out(i).wait_send())


def body(tokens, slot_owner, clip_pieces, clip_length, modulation, qkv_weight, qk_gain, proj_weight):
    vmem = pl.BlockSpec(memory_space=pltpu.VMEM)
    smem = pl.BlockSpec(memory_space=pltpu.SMEM)
    dma = pltpu.SemaphoreType.DMA
    result = pl.pallas_call(
        kernel,
        out_shape=jax.ShapeDtypeStruct((ROWS, D), BF16),
        in_specs=[vmem, vmem, vmem, smem, vmem, vmem, vmem, vmem],
        out_specs=vmem,
        scratch_shapes=[
            pltpu.VMEM((N_DP, 8, D), BF16),
            pltpu.VMEM((N_DP, 8, D), BF16),
            pltpu.VMEM((CHUNKS, NY, CHUNK_ROWS, D), BF16),
            pltpu.VMEM((NX, 2, 3, HD, HALF), BF16),
            pltpu.VMEM((NX * 3 * HD, D), BF16),
            pltpu.VMEM((NX * 3 * HD, ROWS), F32),
            pltpu.VMEM((2, N_SEQ, HD, HALF), BF16),
            pltpu.VMEM((N_SEQ * HD, D), BF16),
            pltpu.VMEM((CHUNKS, NX, 3, HD, ROWS), BF16),
            pltpu.VMEM((NX, CHUNKS, 3, HD, ROWS), BF16),
            pltpu.VMEM((CLIPS, 8, HD, 128), BF16),
            pltpu.VMEM((CLIPS, 8, 128, HD), BF16),
            pltpu.VMEM((CLIPS, 8, HD + 8, 128), BF16),
            pltpu.VMEM((CLIPS, 8, HD, 128), BF16),
            pltpu.VMEM((N_SEQ, HD, ROWS), BF16),
            pltpu.VMEM((N_SEQ, HD, ROWS), BF16),
            pltpu.VMEM((N_DP, 8, D), BF16),
            pltpu.VMEM((N_DP, 8, D), BF16),
            pltpu.VMEM((512, 512), BF16),
            pltpu.VMEM((512, 512), BF16),
            pltpu.VMEM((ROWS, ROWS), BF16),
            pltpu.VMEM((ROWS, ROWS), BF16),
            pltpu.VMEM((ROWS, 128), I32),
            dma((N_DP,)), dma((N_DP,)),
            dma((CHUNKS, 4)), dma((CHUNKS, 4)), dma((CHUNKS, 4)), dma((CHUNKS, 4)),
            dma((4,)), dma((4,)), dma((4,)), dma((4,)),
            dma((N_SEQ,)), dma((N_SEQ,)), dma((N_SEQ,)), dma((N_SEQ,)), dma((N_SEQ,)), dma((N_SEQ,)),
            dma((N_DP,)), dma((N_DP,)),
            dma((8,)), dma((CHUNKS,)),
        ],
        compiler_params=pltpu.CompilerParams(
            collective_id=0, has_side_effects=True, vmem_limit_bytes=50 * 1024 * 1024
        ),
        cost_estimate=pl.CostEstimate(flops=5 * 10**9, bytes_accessed=4 * 10**6, transcendentals=4 * 10**6),
        name="block",
    )(
        tokens[0].reshape(ROWS, D),
        slot_owner,
        clip_pieces[0],
        clip_length,
        modulation[0].transpose(1, 0, 2),
        qkv_weight.transpose(1, 2, 0),
        qk_gain,
        proj_weight,
    )
    return result.reshape(1, 64, 4, D)


def solution(mesh):
    return jax.shard_map(
        body,
        mesh=mesh,
        in_specs=(
            P("dp", None, "seq", None),
            P("dp", None),
            P("dp", None, None),
            P("dp", None),
            P("dp", None, None, None),
            P(None, None, "seq"),
            P(),
            P("seq", None),
        ),
        out_specs=P("dp", None, "seq", None),
        check_vma=False,
    )
```

time: 280 us -> 136 us (0.49)
  waiting for transfers between devices: 163 us -> 0 us
  Pallas kernels: 0 us -> 133 us
  starting transfers between devices: 42.5 us -> 0 us
  local copies, waits for them, and re-layouts: 27.2 us -> 2.5 us
  matrix products: 17.5 us -> 0 us
  other arithmetic: 15.1 us -> 0 us
  between operations: 13.7 us -> 0.11 us
    pallas_call x0 -> x1, Pallas kernels: none -> 133 us  [body(): pl.pallas_call(kernel, out_shape=jax.ShapeDtypeStruct((ROWS, D), BF16), i...]
    all_to_all x4 -> x0, waiting for transfers between devices: 129 us -> none  [the longest x1 44.7 us: body(): lax.all_to_all(local_triple, 'seq', split_axis=4, concat_axis=2, tiled=True)]
    all_to_all x4 -> x0, starting transfers between devices: 42.3 us -> none  [the longest x1 16.8 us: body(): lax.all_to_all(outgoing, 'dp', split_axis=0, concat_axis=0, tiled=True)]
    all_gather x2 -> x0, waiting for transfers between devices: 32.6 us -> none  [the longest x1 32.6 us: body(): lax.all_gather(qkv_weight, 'seq', axis=2, tiled=True)]
    dot_general x10 -> x0, matrix products: 17.5 us -> none  [the longest x1 6.58 us: body(): jnp.einsum('nd,dtc->ntc', flat_hidden, lax.all_gather(qkv_weight, 'seq',...]
    sort x3 -> x0, other arithmetic: 6.86 us -> none  [the longest x1 2.69 us: body(): sorted_slots = jnp.argsort(slot_owner[0], stable=True)]
    gather x4 -> x0, local copies, waits for them, and re-layouts: 6.65 us -> none  [the longest x1 1.85 us: body(): home_pieces = result.reshape(pieces_here, piece_rows, model_width)[inverse]]
    all_to_all x3 -> x0, local copies, waits for them, and re-layouts: 6.19 us -> none  [the longest x1 5.32 us: body(): lax.all_to_all(local_triple, 'seq', split_axis=4, concat_axis=2, tiled=True)]
  transfers between devices with their start and end apart: 6 -> 0, of which waited for: 5 -> 0; matrix products, arithmetic and copies ran while one was open for 14% -> 0% of each run, Pallas kernels for 0% -> 0%
where the time goes in v1:
time: 136 us
  Pallas kernels  133 us (98%)
  local copies, waits for them, and re-layouts  2.5 us (2%)
    pallas_call x1, Pallas kernels, body(): pl.pallas_call(kernel, out_shape=jax.ShapeDtypeStruct((ROWS, D), BF16), i...  133 us

profile of v1, /device:TPU:1, one launch (start us, length us, event | category | flops | bytes accessed | tf_op | source)
XLA Modules:
  0.0 135.8 jit_solution(1432965090171147500)
XLA Ops:
  0.0 0.0 copy-start
  0.0 0.0 copy-start.1
  0.0 0.0 copy-start.2
  0.0 0.0 copy-start.3
  0.0 0.0 copy-start.4
  0.0 0.0 copy-start.5
  0.0 0.0 copy-start.6
  0.0 1.5 %reshape_squeeze.3.tok = bf16[256,1152]{1,0:T(8,128)(2,1)S(1)} reshape(bf16[1,64,4,1152]{3,2,1,0:T(4,128)(2,1)} %param.8) | data formatting | bytes 1179648 | tf_op jit(solution)/shard_map/reshape;squeeze | solution.py:401
  1.6 0.0 copy-done
  1.6 0.0 copy-done.1
  1.6 0.0 copy-done.2
  1.6 0.0 copy-done.3
  1.6 0.0 copy-done.4
  1.6 0.0 copy-done.5
  1.6 0.0 copy-done.6
  1.6 133.2 %block.1 = bf16[256,1152]{1,0:T(8,128)(2,1)S(1)} custom-call(bf16[256,1152]{1,0:T(8,128)(2,1)S(1)} %reshape_squeeze.3.tok, s32[1,64]{1,0:T(1,128)S(1)} %copy-done.5, s32[4,16]{1,0:T(4,128)S(1)} %bitcast.7, s32[1,4]{1,0:T(1,128)S(1)} %copy-done.6, bf16[3,4,1152]{2,1,0:T(4,128)(2,1)S(1)} %bitcast.6, bf16[3,72,1152]{2,1,0:T(8,128)(2,1)S(1)} %bitcast.5, ...), custom_call_target="tpu_custom_call" | custom-call | flops 5000000000 | bytes 4000000 | tf_op jit(solution)/shard_map/block/pallas_call | solution.py:359
  134.9 1.0 reshape.3
Async XLA Ops:
  0.0 1.6 %copy-start = (bf16[1152,3,72]{0,2,1:T(8,128)(2,1)S(1)}, bf16[1152,3,72]{0,2,1:T(8,128)(2,1)}, u32[]{:S(2)}) copy-start(bf16[1152,3,72]{0,2,1:T(8,128)(2,1)} %param.13) | copy-start | bytes 1492996
  0.0 1.6 %copy-start.1 = (bf16[72,1152]{1,0:T(8,128)(2,1)S(1)}, bf16[72,1152]{1,0:T(8,128)(2,1)}, u32[]{:S(2)}) copy-start(bf16[72,1152]{1,0:T(8,128)(2,1)} %pw.1) | copy-start | bytes 497668
  0.0 1.6 %copy-start.2 = (bf16[1,4,3,1152]{3,1,2,0:T(4,128)(2,1)S(1)}, bf16[1,4,3,1152]{3,1,2,0:T(4,128)(2,1)}, u32[]{:S(2)}) copy-start(bf16[1,4,3,1152]{3,1,2,0:T(4,128)(2,1)} %param.12) | copy-start | bytes 82948
  0.0 1.6 %copy-start.3 = (s32[1,4,16]{2,1,0:T(4,128)S(1)}, s32[1,4,16]{2,1,0:T(4,128)}, u32[]{:S(2)}) copy-start(s32[1,4,16]{2,1,0:T(4,128)} %param.10) | copy-start | bytes 772
  0.0 1.6 %copy-start.4 = (f32[2,72]{1,0:T(2,128)S(1)}, f32[2,72]{1,0:T(2,128)}, u32[]{:S(2)}) copy-start(f32[2,72]{1,0:T(2,128)} %gain.1) | copy-start | bytes 1732
  0.0 1.6 %copy-start.5 = (s32[1,64]{1,0:T(1,128)S(1)}, s32[1,64]{1,0:T(1,128)}, u32[]{:S(2)}) copy-start(s32[1,64]{1,0:T(1,128)} %owner.1) | copy-start | bytes 772
  0.0 1.6 %copy-start.6 = (s32[1,4]{1,0:T(1,128)S(1)}, s32[1,4]{1,0:T(1,128)}, u32[]{:S(2)}) copy-start(s32[1,4]{1,0:T(1,128)} %length.1) | copy-start | bytes 52

commit v2 on v1

--- a/solution.py
+++ b/solution.py
@@ -40,12 +40,11 @@
 
 
 def slot_of(distance):
-    return jnp.where(distance < 16, 2 * (16 - distance) - 1, 2 * (distance - 16))
+    return (distance & (CHUNKS - 1)) * PER_CHUNK + (distance >> 2)
 
 
 def distance_of(slot):
-    k = (slot + 1) // 2
-    return 16 + k * (1 - 2 * (slot % 2))
+    return (slot % PER_CHUNK) * CHUNKS + slot // PER_CHUNK
 
 
 def column_of(row, n):
@@ -58,15 +57,24 @@
     tok, owner, table, length, mod, w, gain, pw, out,
     outgoing, arrived, hid, wall, wcat, res, pwall, pwcat, stage, qkv, qc, kc, vc, att, attsend, attin,
     ret, back, spread, spread_t, unroute, route, clip_col,
-    dp_send, dp_recv, y_send, y_recv, x_send, x_recv, w_send, w_recv, wf_send, wf_recv,
+    dp_send, dp_recv, y_send, y_recv, x_send, x_recv, w_send, w_recv,
     p_send, p_recv, pf_send, pf_recv, a_send, a_recv, r_send, r_recv, local, x_local,
 ):
     me = lax.axis_index("dp")
     sq = lax.axis_index("seq")
     core = me % 2
     sibling = me + 1 - 2 * core
-    y = sq // NX
-    x = sq % NX
+    u = (sq // NX) * (1 - core) + (sq % NX) * core
+    v = (sq % NX) * (1 - core) + (sq // NX) * core
+
+    def seq_at(u_of, v_of):
+        return (u_of * 4 + v_of) * (1 - core) + (v_of * 4 + u_of) * core
+
+    def ahead(position, step):
+        return (position + step) % 4
+
+    def behind(position, step):
+        return (position - step + 4) % 4
 
     def remote(src, dst, send, recv, dp, seq):
         return pltpu.make_async_remote_copy(
@@ -84,36 +92,37 @@
 
     def hid_copy(k, step, row):
         return remote(
-            hid.at[k, row], hid.at[k, row], y_send.at[k, step], y_recv.at[k, step], me, ((y + step) % NY) * NX + x
+            hid.at[k, row], hid.at[k, row], y_send.at[k, step], y_recv.at[k, step], me, seq_at(ahead(u, step), v)
         )
 
     def w_copy(step, col):
-        return remote(
-            wall.at[col, core], wall.at[col, core], w_send.at[step], w_recv.at[step], me, y * NX + (x + step) % NX
-        )
-
-    def w_forward(step, half):
-        col = (x - step + NX) % NX
-        return remote(wall.at[col, half], wall.at[col, half], wf_send.at[step], wf_recv.at[step], sibling, sq)
+        return remote(wall.at[col], wall.at[col], w_send.at[step], w_recv.at[step], me, seq_at(u, ahead(v, step)))
 
     def x_copy(k, step, col):
         return remote(
-            stage.at[k, (x + step) % NX], qkv.at[col, k], x_send.at[k, step], x_recv.at[k, step],
-            me, y * NX + (x + step) % NX,
-        )
-
-    def p_copy(step, head):
+            stage.at[k, ahead(v, step)], qkv.at[col, k], x_send.at[k, step], x_recv.at[k, step],
+            me, seq_at(u, ahead(v, step)),
+        )
+
+    def p_first(step, col):
         return remote(
-            pwall.at[core, head], pwall.at[core, head], p_send.at[step], p_recv.at[step], me, (sq + step) % N_SEQ
-        )
-
-    def p_forward(step, half):
-        head = (sq - step + N_SEQ) % N_SEQ
-        return remote(pwall.at[half, head], pwall.at[half, head], pf_send.at[step], pf_recv.at[step], sibling, sq)
+            pwall.at[core, u, col], pwall.at[core, u, col], p_send.at[0, step], p_recv.at[0, step],
+            me, seq_at(u, ahead(v, step)),
+        )
+
+    def p_second(step, row):
+        return remote(
+            pwall.at[core, row], pwall.at[core, row], p_send.at[1, step], p_recv.at[1, step],
+            me, seq_at(ahead(u, step), v),
+        )
+
+    def p_forward(row, half):
+        return remote(pwall.at[half, row], pwall.at[half, row], pf_send.at[row], pf_recv.at[row], sibling, sq)
 
     def a_copy(step, head):
         to = (sq + step) % N_SEQ
-        return remote(attsend.at[to], attin.at[head], a_send.at[step], a_recv.at[step], me, to)
+        at = to * (1 - core) + ((to % 4) * 4 + to // 4) * core
+        return remote(attsend.at[at], attin.at[head], a_send.at[step], a_recv.at[step], me, to)
 
     def each(first, last, action):
         lax.fori_loop(first, last, lambda i, c: (action(i), c)[1], 0)
@@ -124,13 +133,11 @@
     each(1, N_SEQ, lambda i: pl.semaphore_signal(
         barrier, inc=1, device_id={"dp": me, "seq": (sq + i) % N_SEQ}, device_id_type=MESH))
 
-    own = []
-    for half in range(2):
-        cols = pl.ds(half * REST, HALF)
-        own.append(pltpu.make_async_copy(w.at[:, :, cols], wall.at[x, half], local.at[half]))
-        own.append(pltpu.make_async_copy(pw.at[:, cols], pwall.at[half, sq], local.at[2 + half]))
-    for copy in own:
-        copy.start()
+    cols = pl.ds(pl.multiple_of(core * REST, 128), HALF)
+    own_w = pltpu.make_async_copy(w, wall.at[v], local.at[0])
+    own_p = pltpu.make_async_copy(pw.at[:, cols], pwall.at[core, u, v], local.at[1])
+    own_w.start()
+    own_p.start()
 
     owners = owner[...]
     owners_f = jnp.broadcast_to(owners.astype(F32), (64, 64))
@@ -146,13 +153,20 @@
 
     pl.semaphore_wait(barrier, N_DP - 1 + N_SEQ - 1)
 
-    own[0].wait()
-    own[2].wait()
+    own_w.wait()
+    own_p.wait()
+    self_in = pltpu.make_async_copy(outgoing.at[0], arrived.at[0], local.at[4])
+    self_in.start()
+
+    def tokens_out(k):
+        each(k * PER_CHUNK + (1 if k == 0 else 0), (k + 1) * PER_CHUNK, lambda i: tok_out(i).start())
+
+    tokens_out(0)
     for step in (2, 1, 3):
-        w_copy(step, x).start()
-    each(0, N_DP - 1, lambda i: tok_out(i).start())
-    self_in = pltpu.make_async_copy(outgoing.at[N_DP - 1], arrived.at[N_DP - 1], local.at[4])
-    self_in.start()
+        w_copy(step, v).start()
+    tokens_out(1)
+    for step in (2, 1, 3):
+        p_first(step, v).start()
 
     keys_col = column_of(keys, ROWS)
     route[...] = jnp.where(iota((ROWS, ROWS), 1) == keys_col, 1.0, 0.0).astype(BF16)
@@ -185,21 +199,21 @@
         rows = [factors[c:c + 1, :] for c in range(CLIPS)]
         return jnp.where(clip == 0, rows[0], jnp.where(clip == 1, rows[1], jnp.where(clip == 2, rows[2], rows[3])))
 
-    def chunk_in(k, last):
-        def wait(i):
-            tok_out(i).wait_recv()
-        each(k * PER_CHUNK, (k + 1) * PER_CHUNK - (1 if last else 0), wait)
-        if last:
+    def chunk_in(k):
+        if k == 0:
             self_in.wait()
+        each(k * PER_CHUNK + (1 if k == 0 else 0), (k + 1) * PER_CHUNK, lambda i: tok_out(i).wait_recv())
+        if k + 2 < CHUNKS:
+            tokens_out(k + 2)
         rows = arrived[pl.ds(k * PER_CHUNK, PER_CHUNK)].astype(F32).reshape(CHUNK_ROWS, D)
         clip = clip_col[pl.ds(pl.multiple_of(k * CHUNK_ROWS, CHUNK_ROWS), CHUNK_ROWS), 0:1] >> 6
         centered = rows - jnp.mean(rows, axis=-1, keepdims=True)
         variance = jnp.mean(centered * centered, axis=-1, keepdims=True)
         normed = centered * lax.rsqrt(variance + EPSILON)
         hidden = normed * (1.0 + of_its_clip(clip, 1)) + of_its_clip(clip, 0)
-        hid[k, pl.ds(y, 1)] = hidden.astype(BF16)[None]
+        hid[k, pl.ds(u, 1)] = hidden.astype(BF16)[None]
         for step in (2, 1, 3):
-            hid_copy(k, step, y).start()
+            hid_copy(k, step, u).start()
 
     gains = []
     for i in range(2):
@@ -208,11 +222,11 @@
         gains.append(jnp.sum(picked, axis=1, keepdims=True))
 
     def own_stage(k):
-        return pltpu.make_async_copy(stage.at[k, x], qkv.at[x, k], x_local.at[k])
+        return pltpu.make_async_copy(stage.at[k, v], qkv.at[v, k], x_local.at[k])
 
     def chunk_qkv(k):
         for step in (1, 2, 3):
-            hid_copy(k, step, (y - step + NY) % NY).wait_recv()
+            hid_copy(k, step, behind(u, step)).wait_recv()
         rows = hid[k].reshape(ROWS, D)
         res[...] = mm_nt(wcat[...], rows)
         for head in range(NX):
@@ -223,36 +237,32 @@
                 stage[k, head, part] = (block * lax.rsqrt(mean_square + EPSILON) * gains[part]).astype(BF16)
             stage[k, head, 2] = res[base + 2 * HD:base + 3 * HD, :].astype(BF16)
         for step in (2, 1, 3):
-            x_copy(k, step, x).start()
+            x_copy(k, step, v).start()
         own_stage(k).start()
 
-    chunk_in(0, False)
+    chunk_in(0)
+    chunk_in(1)
     for step in (1, 2, 3):
-        w_copy(step, (x - step + NX) % NX).wait_recv()
-        w_forward(step, core).start()
-    chunk_in(1, False)
-    for step in (1, 2, 3):
-        w_forward(step, 1 - core).wait_recv()
-    for pair in range(NX // 2):
-        rows = slice(pair * 6 * HD, (pair + 1) * 6 * HD)
-        cols = slice(2 * pair, 2 * pair + 2)
-        wcat[rows, 0:HALF] = wall[cols, 0].astype(F32).reshape(6 * HD, HALF).astype(BF16)
-        wcat[rows, HALF:D] = wall[cols, 1].astype(F32).reshape(6 * HD, HALF)[:, HALF - REST:].astype(BF16)
+        w_copy(step, behind(v, step)).wait_recv()
+    for pair in range(2):
+        rows = wall[2 * pair:2 * pair + 2].astype(F32).reshape(6 * HD, D)
+        wcat[pair * 6 * HD:(pair + 1) * 6 * HD, :] = rows.astype(BF16)
     chunk_qkv(0)
-    chunk_in(2, False)
+    chunk_in(2)
     chunk_qkv(1)
-    chunk_in(3, True)
+    chunk_in(3)
     chunk_qkv(2)
     chunk_qkv(3)
 
-    own[1].wait()
-    own[3].wait()
-    each(1, N_SEQ, lambda i: p_copy(i, sq).start())
+    for step in (1, 2, 3):
+        p_first(step, behind(v, step)).wait_recv()
+    for step in (2, 1, 3):
+        p_second(step, u).start()
 
     for k in range(CHUNKS):
         own_stage(k).wait()
         for step in (1, 2, 3):
-            x_copy(k, step, (x - step + NX) % NX).wait_recv()
+            x_copy(k, step, behind(v, step)).wait_recv()
     lane = iota((1, 128), 1)
 
     def to_clips(col, carry):
@@ -267,7 +277,8 @@
                 cut = slice(clip * 128, (clip + 1) * 128)
                 qc[clip, col * 2 + pair] = queries[:, cut]
                 kc[clip, col * 2 + pair] = keys_of[cut, :]
-                position = ((lane >> 2) & 15) * 64 + ((pair * 2 + (lane >> 6)) * NX + col) * 4 + (lane & 3)
+                holder = jnp.where(lane < 64, seq_at(pair * 2, col), seq_at(pair * 2 + 1, col))
+                position = ((lane >> 2) & 15) * 64 + holder * 4 + (lane & 3)
                 inside = jnp.where(position < length[0, clip], 1.0, 0.0)
                 ones = jnp.broadcast_to(inside, (8, 128))
                 vc[clip, col * 2 + pair] = jnp.concatenate([values[:, cut] * inside, ones], axis=0).astype(BF16)
@@ -290,10 +301,11 @@
             att[clip, 2 * block + 1] = attended[:, 128:256]
         return carry
 
-    lax.fori_loop(0, 2, attend, 0)
-    each(1, N_SEQ, lambda i: p_copy(i, (sq - i + N_SEQ) % N_SEQ).wait_recv())
-    each(1, N_SEQ, lambda i: p_forward(i, core).start())
-    lax.fori_loop(2, CLIPS, attend, 0)
+    lax.fori_loop(0, 3, attend, 0)
+    for step in (1, 2, 3):
+        p_second(step, behind(u, step)).wait_recv()
+    each(0, 4, lambda i: p_forward(i, core).start())
+    lax.fori_loop(3, CLIPS, attend, 0)
 
     come = iota((512, 512), 0)
     go = iota((512, 512), 1)
@@ -302,17 +314,19 @@
         blocks = jnp.concatenate([att[clip, pair] for clip in range(CLIPS)], axis=1)
         swapped = mm(blocks, swap).astype(BF16)
         for half in range(2):
-            attsend[((pair % 2) * 2 + half) * NX + pair // 2] = swapped[:, half * ROWS:(half + 1) * ROWS]
+            attsend[((pair % 2) * 2 + half) * 4 + pair // 2] = swapped[:, half * ROWS:(half + 1) * ROWS]
     each(1, N_SEQ, lambda i: a_copy(i, sq).start())
-    self_att = pltpu.make_async_copy(attsend.at[sq], attin.at[sq], local.at[5])
+    self_att = pltpu.make_async_copy(attsend.at[u * 4 + v], attin.at[sq], local.at[5])
     self_att.start()
 
-    each(1, N_SEQ, lambda i: p_forward(i, 1 - core).wait_recv())
-    for head in range(N_SEQ // 2):
-        rows = pl.ds(head * 2 * HD, 2 * HD)
-        pwcat[rows, 0:HALF] = pwall[0, 2 * head:2 * head + 2].astype(F32).reshape(2 * HD, HALF).astype(BF16)
-        pwcat[rows, HALF:D] = (
-            pwall[1, 2 * head:2 * head + 2].astype(F32).reshape(2 * HD, HALF)[:, HALF - REST:].astype(BF16))
+    each(0, 4, lambda i: p_forward(i, 1 - core).wait_recv())
+    for pair in range(N_SEQ // 2):
+        rows = pl.ds(pair * 2 * HD, 2 * HD)
+        row, col = pair // 2, (pair % 2) * 2
+        left = jnp.concatenate([pwall[0, row, col].astype(F32), pwall[0, row, col + 1].astype(F32)], axis=0)
+        right = jnp.concatenate([pwall[1, col, row].astype(F32), pwall[1, col + 1, row].astype(F32)], axis=0)
+        pwcat[rows, 0:HALF] = left.astype(BF16)
+        pwcat[rows, HALF:D] = right[:, HALF - REST:].astype(BF16)
 
     self_att.wait()
     each(1, N_SEQ, lambda i: a_copy(i, (sq - i + N_SEQ) % N_SEQ).wait_recv())
@@ -330,26 +344,26 @@
         rows = arrived[part * 16:(part + 1) * 16].astype(F32).reshape(half_rows, D)
         result = jnp.where(position < limit, rows + of_its_clip(clip, 2) * branch, 0.0)
         ret[part * 16:(part + 1) * 16] = result.reshape(16, 8, D).astype(BF16)
-        each(part * 16, part * 16 + 16 - part, lambda i: ret_out(i).start())
-    self_back = pltpu.make_async_copy(ret.at[N_DP - 1], back.at[N_DP - 1], local.at[6])
+        each(part * 16 + 1 - part, part * 16 + 16, lambda i: ret_out(i).start())
+    self_back = pltpu.make_async_copy(ret.at[0], back.at[0], local.at[6])
     self_back.start()
 
     for step in (1, 2, 3):
-        w_copy(step, x).wait_send()
-        w_forward(step, core).wait_send()
+        w_copy(step, v).wait_send()
+        p_first(step, v).wait_send()
+        p_second(step, u).wait_send()
         for k in range(CHUNKS):
-            hid_copy(k, step, y).wait_send()
-            x_copy(k, step, x).wait_send()
-    each(0, N_DP - 1, lambda i: tok_out(i).wait_send())
-    each(1, N_SEQ, lambda i: p_copy(i, sq).wait_send())
-    each(1, N_SEQ, lambda i: p_forward(i, core).wait_send())
+            hid_copy(k, step, u).wait_send()
+            x_copy(k, step, v).wait_send()
+    each(1, N_DP, lambda i: tok_out(i).wait_send())
+    each(0, 4, lambda i: p_forward(i, core).wait_send())
     each(1, N_SEQ, lambda i: a_copy(i, sq).wait_send())
 
     self_back.wait()
-    each(0, N_DP - 1, lambda i: ret_out(i).wait_recv())
+    each(1, N_DP, lambda i: ret_out(i).wait_recv())
     returned = back[...].astype(F32).reshape(ROWS, D).astype(BF16)
     out[...] = mm(route[...], returned).astype(BF16)
-    each(0, N_DP - 1, lambda i: ret_out(i).wait_send())
+    each(1, N_DP, lambda i: ret_out(i).wait_send())
 
 
 def body(tokens, slot_owner, clip_pieces, clip_length, modulation, qkv_weight, qk_gain, proj_weight):
@@ -365,10 +379,10 @@
             pltpu.VMEM((N_DP, 8, D), BF16),
             pltpu.VMEM((N_DP, 8, D), BF16),
             pltpu.VMEM((CHUNKS, NY, CHUNK_ROWS, D), BF16),
-            pltpu.VMEM((NX, 2, 3, HD, HALF), BF16),
+            pltpu.VMEM((NX, 3, HD, D), BF16),
             pltpu.VMEM((NX * 3 * HD, D), BF16),
             pltpu.VMEM((NX * 3 * HD, ROWS), F32),
-            pltpu.VMEM((2, N_SEQ, HD, HALF), BF16),
+            pltpu.VMEM((2, 4, 4, HD, HALF), BF16),
             pltpu.VMEM((N_SEQ * HD, D), BF16),
             pltpu.VMEM((CHUNKS, NX, 3, HD, ROWS), BF16),
             pltpu.VMEM((NX, CHUNKS, 3, HD, ROWS), BF16),
@@ -387,8 +401,8 @@
             pltpu.VMEM((ROWS, 128), I32),
             dma((N_DP,)), dma((N_DP,)),
             dma((CHUNKS, 4)), dma((CHUNKS, 4)), dma((CHUNKS, 4)), dma((CHUNKS, 4)),
-            dma((4,)), dma((4,)), dma((4,)), dma((4,)),
-            dma((N_SEQ,)), dma((N_SEQ,)), dma((N_SEQ,)), dma((N_SEQ,)), dma((N_SEQ,)), dma((N_SEQ,)),
+            dma((4,)), dma((4,)),
+            dma((2, 4)), dma((2, 4)), dma((4,)), dma((4,)), dma((N_SEQ,)), dma((N_SEQ,)),
             dma((N_DP,)), dma((N_DP,)),
             dma((8,)), dma((CHUNKS,)),
         ],

time: 136 us -> 116 us (0.85)
  Pallas kernels: 133 us -> 113 us
    pallas_call x1, Pallas kernels: 133 us -> 113 us  [body(): pl.pallas_call(kernel, out_shape=jax.ShapeDtypeStruct((ROWS, D), BF16), i...]
where the time goes in v2:
time: 116 us; the launch traced here: 115 us
  Pallas kernels  113 us (97%)
  local copies, waits for them, and re-layouts  2.5 us (2%)
    pallas_call x1, Pallas kernels, body(): pl.pallas_call(kernel, out_shape=jax.ShapeDtypeStruct((ROWS, D), BF16), i...  113 us

profile of v2, /device:TPU:1, one launch (start us, length us, event | category | flops | bytes accessed | tf_op | source)
XLA Modules:
  0.0 115.3 jit_solution(6727684398716519927)
XLA Ops:
  0.0 0.0 copy-start
  0.0 0.0 copy-start.1
  0.0 0.0 copy-start.2
  0.0 0.0 copy-start.3
  0.0 0.0 copy-start.4
  0.0 0.0 copy-start.5
  0.0 0.0 copy-start.6
  0.0 1.5 %reshape_squeeze.3.tok = bf16[256,1152]{1,0:T(8,128)(2,1)S(1)} reshape(bf16[1,64,4,1152]{3,2,1,0:T(4,128)(2,1)} %param.8) | data formatting | bytes 1179648 | tf_op jit(solution)/shard_map/reshape;squeeze | solution.py:415
  1.6 0.0 copy-done
  1.6 0.0 copy-done.1
  1.6 0.0 copy-done.2
  1.6 0.0 copy-done.3
  1.6 0.0 copy-done.4
  1.6 0.0 copy-done.5
  1.6 0.0 copy-done.6
  1.6 112.7 %block.1 = bf16[256,1152]{1,0:T(8,128)(2,1)S(1)} custom-call(bf16[256,1152]{1,0:T(8,128)(2,1)S(1)} %reshape_squeeze.3.tok, s32[1,64]{1,0:T(1,128)S(1)} %copy-done.5, s32[4,16]{1,0:T(4,128)S(1)} %bitcast.7, s32[1,4]{1,0:T(1,128)S(1)} %copy-done.6, bf16[3,4,1152]{2,1,0:T(4,128)(2,1)S(1)} %bitcast.6, bf16[3,72,1152]{2,1,0:T(8,128)(2,1)S(1)} %bitcast.5, ...), custom_call_target="tpu_custom_call" | custom-call | flops 5000000000 | bytes 4000000 | tf_op jit(solution)/shard_map/block/pallas_call | solution.py:373
  114.3 1.0 reshape.3
Async XLA Ops:
  0.0 1.6 %copy-start = (bf16[1152,3,72]{0,2,1:T(8,128)(2,1)S(1)}, bf16[1152,3,72]{0,2,1:T(8,128)(2,1)}, u32[]{:S(2)}) copy-start(bf16[1152,3,72]{0,2,1:T(8,128)(2,1)} %param.13) | copy-start | bytes 1492996
  0.0 1.6 %copy-start.1 = (bf16[72,1152]{1,0:T(8,128)(2,1)S(1)}, bf16[72,1152]{1,0:T(8,128)(2,1)}, u32[]{:S(2)}) copy-start(bf16[72,1152]{1,0:T(8,128)(2,1)} %pw.1) | copy-start | bytes 497668
  0.0 1.6 %copy-start.2 = (bf16[1,4,3,1152]{3,1,2,0:T(4,128)(2,1)S(1)}, bf16[1,4,3,1152]{3,1,2,0:T(4,128)(2,1)}, u32[]{:S(2)}) copy-start(bf16[1,4,3,1152]{3,1,2,0:T(4,128)(2,1)} %param.12) | copy-start | bytes 82948
  0.0 1.6 %copy-start.3 = (s32[1,4,16]{2,1,0:T(4,128)S(1)}, s32[1,4,16]{2,1,0:T(4,128)}, u32[]{:S(2)}) copy-start(s32[1,4,16]{2,1,0:T(4,128)} %param.10) | copy-start | bytes 772
  0.0 1.6 %copy-start.4 = (f32[2,72]{1,0:T(2,128)S(1)}, f32[2,72]{1,0:T(2,128)}, u32[]{:S(2)}) copy-start(f32[2,72]{1,0:T(2,128)} %gain.1) | copy-start | bytes 1732
  0.0 1.6 %copy-start.5 = (s32[1,64]{1,0:T(1,128)S(1)}, s32[1,64]{1,0:T(1,128)}, u32[]{:S(2)}) copy-start(s32[1,64]{1,0:T(1,128)} %owner.1) | copy-start | bytes 772
  0.0 1.6 %copy-start.6 = (s32[1,4]{1,0:T(1,128)S(1)}, s32[1,4]{1,0:T(1,128)}, u32[]{:S(2)}) copy-start(s32[1,4]{1,0:T(1,128)} %length.1) | copy-start | bytes 52

commit v3 on v2

--- a/solution.py
+++ b/solution.py
@@ -39,12 +39,12 @@
     return lax.dot_general(a, b, (((1,), (1,)), ((), ())), preferred_element_type=F32)
 
 
-def slot_of(distance):
-    return (distance & (CHUNKS - 1)) * PER_CHUNK + (distance >> 2)
-
-
-def distance_of(slot):
-    return (slot % PER_CHUNK) * CHUNKS + slot // PER_CHUNK
+def out_slot(distance, owner_core):
+    return owner_core * 16 + (distance & 3) * 4 + (distance >> 2)
+
+
+def in_slot(distance, source_core):
+    return (distance & 3) * PER_CHUNK + (distance >> 2) * 2 + source_core
 
 
 def column_of(row, n):
@@ -57,18 +57,24 @@
     tok, owner, table, length, mod, w, gain, pw, out,
     outgoing, arrived, hid, wall, wcat, res, pwall, pwcat, stage, qkv, qc, kc, vc, att, attsend, attin,
     ret, back, spread, spread_t, unroute, route, clip_col,
-    dp_send, dp_recv, y_send, y_recv, x_send, x_recv, w_send, w_recv,
+    dp_send, dp_recv, y_send, y_recv, x_send, x_recv, w_send, w_recv, wf_send, wf_recv,
     p_send, p_recv, pf_send, pf_recv, a_send, a_recv, r_send, r_recv, local, x_local,
 ):
     me = lax.axis_index("dp")
     sq = lax.axis_index("seq")
     core = me % 2
     sibling = me + 1 - 2 * core
-    u = (sq // NX) * (1 - core) + (sq % NX) * core
-    v = (sq % NX) * (1 - core) + (sq // NX) * core
+    z = me // 2
+    u = sq // NX
+    v = sq % NX
+    pu = v * (1 - core) + u * core
+    pv = u * (1 - core) + v * core
 
     def seq_at(u_of, v_of):
-        return (u_of * 4 + v_of) * (1 - core) + (v_of * 4 + u_of) * core
+        return u_of * NX + v_of
+
+    def p_at(u_of, v_of):
+        return (v_of * NX + u_of) * (1 - core) + (u_of * NX + v_of) * core
 
     def ahead(position, step):
         return (position + step) % 4
@@ -83,12 +89,25 @@
         )
 
     def tok_out(i):
-        return remote(outgoing.at[i], arrived.at[i], dp_send.at[i], dp_recv.at[i], (me + distance_of(i)) % N_DP, sq)
-
-    def ret_out(i):
-        return remote(
-            ret.at[i], back.at[i], r_send.at[i], r_recv.at[i], (me - distance_of(i) + N_DP) % N_DP, sq
-        )
+        rank = i % 16
+        distance = (rank % 4) * 4 + rank // 4
+        to = (distance % 4) * PER_CHUNK + (distance // 4) * 2 + core
+        return remote(
+            outgoing.at[i], arrived.at[to], dp_send.at[i], dp_recv.at[to], ((z + distance) % 16) * 2 + i // 16, sq
+        )
+
+    def tok_in(slot):
+        return remote(outgoing.at[slot], arrived.at[slot], dp_send.at[slot], dp_recv.at[slot], sibling, sq)
+
+    def ret_out(slot):
+        distance = slot // PER_CHUNK + ((slot % PER_CHUNK) // 2) * 4
+        to = core * 16 + (distance % 4) * 4 + distance // 4
+        return remote(
+            ret.at[slot], back.at[to], r_send.at[slot], r_recv.at[to], ((z - distance + 16) % 16) * 2 + slot % 2, sq
+        )
+
+    def ret_in(slot):
+        return remote(ret.at[slot], back.at[slot], r_send.at[slot], r_recv.at[slot], sibling, sq)
 
     def hid_copy(k, step, row):
         return remote(
@@ -98,6 +117,10 @@
     def w_copy(step, col):
         return remote(wall.at[col], wall.at[col], w_send.at[step], w_recv.at[step], me, seq_at(u, ahead(v, step)))
 
+    def w_forward(step):
+        col = behind(v, step)
+        return remote(wall.at[col], wall.at[col], wf_send.at[step], wf_recv.at[step], sibling, sq)
+
     def x_copy(k, step, col):
         return remote(
             stage.at[k, ahead(v, step)], qkv.at[col, k], x_send.at[k, step], x_recv.at[k, step],
@@ -106,14 +129,14 @@
 
     def p_first(step, col):
         return remote(
-            pwall.at[core, u, col], pwall.at[core, u, col], p_send.at[0, step], p_recv.at[0, step],
-            me, seq_at(u, ahead(v, step)),
+            pwall.at[core, pu, col], pwall.at[core, pu, col], p_send.at[0, step], p_recv.at[0, step],
+            me, p_at(pu, ahead(pv, step)),
         )
 
     def p_second(step, row):
         return remote(
             pwall.at[core, row], pwall.at[core, row], p_send.at[1, step], p_recv.at[1, step],
-            me, seq_at(ahead(u, step), v),
+            me, p_at(ahead(pu, step), pv),
         )
 
     def p_forward(row, half):
@@ -121,11 +144,16 @@
 
     def a_copy(step, head):
         to = (sq + step) % N_SEQ
-        at = to * (1 - core) + ((to % 4) * 4 + to // 4) * core
-        return remote(attsend.at[at], attin.at[head], a_send.at[step], a_recv.at[step], me, to)
+        return remote(attsend.at[to], attin.at[head], a_send.at[step], a_recv.at[step], me, to)
 
     def each(first, last, action):
         lax.fori_loop(first, last, lambda i, c: (action(i), c)[1], 0)
+
+    def on_core(which, *actions):
+        @pl.when(core == which)
+        def _():
+            for action in actions:
+                action()
 
     barrier = pltpu.get_barrier_semaphore()
     each(1, N_DP, lambda i: pl.semaphore_signal(
@@ -135,7 +163,7 @@
 
     cols = pl.ds(pl.multiple_of(core * REST, 128), HALF)
     own_w = pltpu.make_async_copy(w, wall.at[v], local.at[0])
-    own_p = pltpu.make_async_copy(pw.at[:, cols], pwall.at[core, u, v], local.at[1])
+    own_p = pltpu.make_async_copy(pw.at[:, cols], pwall.at[core, pu, pv], local.at[1])
     own_w.start()
     own_p.start()
 
@@ -144,7 +172,7 @@
     owners_col = column_of(owners, 64).astype(F32)
     earlier = (owners_col == owners_f) & (iota((64, 64), 0) < iota((64, 64), 1))
     rank = jnp.sum(jnp.where(earlier, 1.0, 0.0), axis=0, keepdims=True).astype(I32)
-    piece_key = slot_of((owners - me + N_DP) & (N_DP - 1)) * 8 + rank * 4
+    piece_key = out_slot(((owners >> 1) - z + 16) & 15, owners & 1) * 8 + rank * 4
     widen = jnp.where((iota((64, ROWS), 1) >> 2) == iota((64, ROWS), 0), 1.0, 0.0).astype(BF16)
     keys = mm(jnp.broadcast_to(piece_key.astype(F32), (16, 64)).astype(BF16), widen)[0:1].astype(I32)
     keys = keys + (iota((1, ROWS), 1) & 3)
@@ -155,25 +183,22 @@
 
     own_w.wait()
     own_p.wait()
-    self_in = pltpu.make_async_copy(outgoing.at[0], arrived.at[0], local.at[4])
+    self_in = pltpu.make_async_copy(outgoing.at[core * 16], arrived.at[core], local.at[4])
     self_in.start()
-
-    def tokens_out(k):
-        each(k * PER_CHUNK + (1 if k == 0 else 0), (k + 1) * PER_CHUNK, lambda i: tok_out(i).start())
-
-    tokens_out(0)
+    to_sibling = tok_out((1 - core) * 16)
+
+    each(1, 16, lambda i: tok_out(i).start())
+    to_sibling.start()
     for step in (2, 1, 3):
-        w_copy(step, v).start()
-    tokens_out(1)
-    for step in (2, 1, 3):
-        p_first(step, v).start()
+        p_first(step, pv).start()
+    on_core(0, lambda: [w_copy(step, v).start() for step in (2, 1, 3)])
 
     keys_col = column_of(keys, ROWS)
     route[...] = jnp.where(iota((ROWS, ROWS), 1) == keys_col, 1.0, 0.0).astype(BF16)
 
     def arrival_row(pieces, row):
         source, rank_of = pieces >> 1, pieces & 1
-        return slot_of((me - source + N_DP) & (N_DP - 1)) * 8 + rank_of * 4 + row
+        return in_slot((z - (source >> 1) + 16) & 15, source & 1) * 8 + rank_of * 4 + row
 
     def table_row(width, clip_shift):
         lane = iota((16, width), 1)
@@ -202,9 +227,8 @@
     def chunk_in(k):
         if k == 0:
             self_in.wait()
-        each(k * PER_CHUNK + (1 if k == 0 else 0), (k + 1) * PER_CHUNK, lambda i: tok_out(i).wait_recv())
-        if k + 2 < CHUNKS:
-            tokens_out(k + 2)
+            tok_in(1 - core).wait_recv()
+        each(k * PER_CHUNK + (2 if k == 0 else 0), (k + 1) * PER_CHUNK, lambda i: tok_in(i).wait_recv())
         rows = arrived[pl.ds(k * PER_CHUNK, PER_CHUNK)].astype(F32).reshape(CHUNK_ROWS, D)
         clip = clip_col[pl.ds(pl.multiple_of(k * CHUNK_ROWS, CHUNK_ROWS), CHUNK_ROWS), 0:1] >> 6
         centered = rows - jnp.mean(rows, axis=-1, keepdims=True)
@@ -240,24 +264,44 @@
             x_copy(k, step, v).start()
         own_stage(k).start()
 
+    def second_batch():
+        each(17, N_DP, lambda i: tok_out(i).start())
+
+    def rest_of_projection():
+        for step in (1, 2, 3):
+            p_first(step, behind(pv, step)).wait_recv()
+        for step in (2, 1, 3):
+            p_second(step, pu).start()
+
+    def hand_over():
+        for step in (1, 2, 3):
+            p_second(step, behind(pu, step)).wait_recv()
+        each(0, 4, lambda i: p_forward(i, core).start())
+
+    on_core(1, lambda: each(1, 16, lambda i: tok_out(i).wait_send()), second_batch)
     chunk_in(0)
+    on_core(0, second_batch)
+
+    def weights_in():
+        for step in (1, 2, 3):
+            w_copy(step, behind(v, step)).wait_recv()
+            w_forward(step).start()
+
     chunk_in(1)
-    for step in (1, 2, 3):
-        w_copy(step, behind(v, step)).wait_recv()
+    on_core(0, weights_in, rest_of_projection)
+    chunk_in(2)
+    chunk_in(3)
+    on_core(1, rest_of_projection)
+
+    on_core(1, lambda: [w_forward(step).wait_recv() for step in (1, 2, 3)])
     for pair in range(2):
         rows = wall[2 * pair:2 * pair + 2].astype(F32).reshape(6 * HD, D)
         wcat[pair * 6 * HD:(pair + 1) * 6 * HD, :] = rows.astype(BF16)
     chunk_qkv(0)
-    chunk_in(2)
     chunk_qkv(1)
-    chunk_in(3)
     chunk_qkv(2)
     chunk_qkv(3)
-
-    for step in (1, 2, 3):
-        p_first(step, behind(v, step)).wait_recv()
-    for step in (2, 1, 3):
-        p_second(step, u).start()
+    on_core(0, hand_over)
 
     for k in range(CHUNKS):
         own_stage(k).wait()
@@ -285,6 +329,7 @@
         return carry
 
     lax.fori_loop(0, NX, to_clips, 0)
+    on_core(1, hand_over)
 
     factor = math.log2(math.e) / math.sqrt(HD)
 
@@ -301,11 +346,7 @@
             att[clip, 2 * block + 1] = attended[:, 128:256]
         return carry
 
-    lax.fori_loop(0, 3, attend, 0)
-    for step in (1, 2, 3):
-        p_second(step, behind(u, step)).wait_recv()
-    each(0, 4, lambda i: p_forward(i, core).start())
-    lax.fori_loop(3, CLIPS, attend, 0)
+    lax.fori_loop(0, CLIPS, attend, 0)
 
     come = iota((512, 512), 0)
     go = iota((512, 512), 1)
@@ -316,15 +357,15 @@
         for half in range(2):
             attsend[((pair % 2) * 2 + half) * 4 + pair // 2] = swapped[:, half * ROWS:(half + 1) * ROWS]
     each(1, N_SEQ, lambda i: a_copy(i, sq).start())
-    self_att = pltpu.make_async_copy(attsend.at[u * 4 + v], attin.at[sq], local.at[5])
+    self_att = pltpu.make_async_copy(attsend.at[sq], attin.at[sq], local.at[5])
     self_att.start()
 
     each(0, 4, lambda i: p_forward(i, 1 - core).wait_recv())
     for pair in range(N_SEQ // 2):
         rows = pl.ds(pair * 2 * HD, 2 * HD)
         row, col = pair // 2, (pair % 2) * 2
-        left = jnp.concatenate([pwall[0, row, col].astype(F32), pwall[0, row, col + 1].astype(F32)], axis=0)
-        right = jnp.concatenate([pwall[1, col, row].astype(F32), pwall[1, col + 1, row].astype(F32)], axis=0)
+        left = jnp.concatenate([pwall[0, col, row].astype(F32), pwall[0, col + 1, row].astype(F32)], axis=0)
+        right = jnp.concatenate([pwall[1, row, col].astype(F32), pwall[1, row, col + 1].astype(F32)], axis=0)
         pwcat[rows, 0:HALF] = left.astype(BF16)
         pwcat[rows, HALF:D] = right[:, HALF - REST:].astype(BF16)
 
@@ -344,26 +385,37 @@
         rows = arrived[part * 16:(part + 1) * 16].astype(F32).reshape(half_rows, D)
         result = jnp.where(position < limit, rows + of_its_clip(clip, 2) * branch, 0.0)
         ret[part * 16:(part + 1) * 16] = result.reshape(16, 8, D).astype(BF16)
-        each(part * 16 + 1 - part, part * 16 + 16, lambda i: ret_out(i).start())
-    self_back = pltpu.make_async_copy(ret.at[0], back.at[0], local.at[6])
+        each(part * 16 + 2 * (1 - part), part * 16 + 16, lambda i: ret_out(i).start())
+    ret_out(1 - core).start()
+    self_back = pltpu.make_async_copy(ret.at[core], back.at[core * 16], local.at[6])
     self_back.start()
 
     for step in (1, 2, 3):
-        w_copy(step, v).wait_send()
-        p_first(step, v).wait_send()
-        p_second(step, u).wait_send()
+        p_first(step, pv).wait_send()
+        p_second(step, pu).wait_send()
         for k in range(CHUNKS):
             hid_copy(k, step, u).wait_send()
             x_copy(k, step, v).wait_send()
-    each(1, N_DP, lambda i: tok_out(i).wait_send())
+    @pl.when(core == 0)
+    def _():
+        each(1, 16, lambda i: tok_out(i).wait_send())
+        for step in (1, 2, 3):
+            w_copy(step, v).wait_send()
+            w_forward(step).wait_send()
+
+    to_sibling.wait_send()
+    each(17, N_DP, lambda i: tok_out(i).wait_send())
     each(0, 4, lambda i: p_forward(i, core).wait_send())
     each(1, N_SEQ, lambda i: a_copy(i, sq).wait_send())
 
     self_back.wait()
-    each(1, N_DP, lambda i: ret_out(i).wait_recv())
+    ret_in((1 - core) * 16).wait_recv()
+    each(1, 16, lambda i: ret_in(i).wait_recv())
+    each(17, N_DP, lambda i: ret_in(i).wait_recv())
     returned = back[...].astype(F32).reshape(ROWS, D).astype(BF16)
     out[...] = mm(route[...], returned).astype(BF16)
-    each(1, N_DP, lambda i: ret_out(i).wait_send())
+    ret_out(1 - core).wait_send()
+    each(2, N_DP, lambda i: ret_out(i).wait_send())
 
 
 def body(tokens, slot_owner, clip_pieces, clip_length, modulation, qkv_weight, qk_gain, proj_weight):
@@ -401,7 +453,7 @@
             pltpu.VMEM((ROWS, 128), I32),
             dma((N_DP,)), dma((N_DP,)),
             dma((CHUNKS, 4)), dma((CHUNKS, 4)), dma((CHUNKS, 4)), dma((CHUNKS, 4)),
-            dma((4,)), dma((4,)),
+            dma((4,)), dma((4,)), dma((4,)), dma((4,)),
             dma((2, 4)), dma((2, 4)), dma((4,)), dma((4,)), dma((N_SEQ,)), dma((N_SEQ,)),
             dma((N_DP,)), dma((N_DP,)),
             dma((8,)), dma((CHUNKS,)),

time: 116 us -> 110 us (0.948)
  Pallas kernels: 113 us -> 107 us
    pallas_call x1, Pallas kernels: 113 us -> 107 us  [body(): pl.pallas_call(kernel, out_shape=jax.ShapeDtypeStruct((ROWS, D), BF16), i...]
where the time goes in v3:
time: 110 us; the launch traced here: 109 us
  Pallas kernels  107 us (97%)
  local copies, waits for them, and re-layouts  2.5 us (2%)
    pallas_call x1, Pallas kernels, body(): pl.pallas_call(kernel, out_shape=jax.ShapeDtypeStruct((ROWS, D), BF16), i...  107 us

profile of v3, /device:TPU:1, one launch (start us, length us, event | category | flops | bytes accessed | tf_op | source)
XLA Modules:
  0.0 109.4 jit_solution(9230298545844032800)
XLA Ops:
  0.0 0.0 copy-start
  0.0 0.0 copy-start.1
  0.0 0.0 copy-start.2
  0.0 0.0 copy-start.3
  0.0 0.0 copy-start.4
  0.0 0.0 copy-start.5
  0.0 0.0 copy-start.6
  0.0 1.5 %reshape_squeeze.3.tok = bf16[256,1152]{1,0:T(8,128)(2,1)S(1)} reshape(bf16[1,64,4,1152]{3,2,1,0:T(4,128)(2,1)} %param.8) | data formatting | bytes 1179648 | tf_op jit(solution)/shard_map/reshape;squeeze | solution.py:467
  1.6 0.0 copy-done
  1.6 0.0 copy-done.1
  1.6 0.0 copy-done.2
  1.6 0.0 copy-done.3
  1.6 0.0 copy-done.4
  1.6 0.0 copy-done.5
  1.6 0.0 copy-done.6
  1.6 106.8 %block.1 = bf16[256,1152]{1,0:T(8,128)(2,1)S(1)} custom-call(bf16[256,1152]{1,0:T(8,128)(2,1)S(1)} %reshape_squeeze.3.tok, s32[1,64]{1,0:T(1,128)S(1)} %copy-done.5, s32[4,16]{1,0:T(4,128)S(1)} %bitcast.7, s32[1,4]{1,0:T(1,128)S(1)} %copy-done.6, bf16[3,4,1152]{2,1,0:T(4,128)(2,1)S(1)} %bitcast.6, bf16[3,72,1152]{2,1,0:T(8,128)(2,1)S(1)} %bitcast.5, ...), custom_call_target="tpu_custom_call" | custom-call | flops 5000000000 | bytes 4000000 | tf_op jit(solution)/shard_map/block/pallas_call | solution.py:425
  108.4 1.0 reshape.3
Async XLA Ops:
  0.0 1.6 %copy-start = (bf16[1152,3,72]{0,2,1:T(8,128)(2,1)S(1)}, bf16[1152,3,72]{0,2,1:T(8,128)(2,1)}, u32[]{:S(2)}) copy-start(bf16[1152,3,72]{0,2,1:T(8,128)(2,1)} %param.13) | copy-start | bytes 1492996
  0.0 1.6 %copy-start.1 = (bf16[72,1152]{1,0:T(8,128)(2,1)S(1)}, bf16[72,1152]{1,0:T(8,128)(2,1)}, u32[]{:S(2)}) copy-start(bf16[72,1152]{1,0:T(8,128)(2,1)} %pw.1) | copy-start | bytes 497668
  0.0 1.6 %copy-start.2 = (bf16[1,4,3,1152]{3,1,2,0:T(4,128)(2,1)S(1)}, bf16[1,4,3,1152]{3,1,2,0:T(4,128)(2,1)}, u32[]{:S(2)}) copy-start(bf16[1,4,3,1152]{3,1,2,0:T(4,128)(2,1)} %param.12) | copy-start | bytes 82948
  0.0 1.6 %copy-start.3 = (s32[1,4,16]{2,1,0:T(4,128)S(1)}, s32[1,4,16]{2,1,0:T(4,128)}, u32[]{:S(2)}) copy-start(s32[1,4,16]{2,1,0:T(4,128)} %param.10) | copy-start | bytes 772
  0.0 1.6 %copy-start.4 = (f32[2,72]{1,0:T(2,128)S(1)}, f32[2,72]{1,0:T(2,128)}, u32[]{:S(2)}) copy-start(f32[2,72]{1,0:T(2,128)} %gain.1) | copy-start | bytes 1732
  0.0 1.6 %copy-start.5 = (s32[1,64]{1,0:T(1,128)S(1)}, s32[1,64]{1,0:T(1,128)}, u32[]{:S(2)}) copy-start(s32[1,64]{1,0:T(1,128)} %owner.1) | copy-start | bytes 772
  0.0 1.6 %copy-start.6 = (s32[1,4]{1,0:T(1,128)S(1)}, s32[1,4]{1,0:T(1,128)}, u32[]{:S(2)}) copy-start(s32[1,4]{1,0:T(1,128)} %length.1) | copy-start | bytes 52

commit v4 on v3

--- a/solution.py
+++ b/solution.py
@@ -142,9 +142,9 @@
     def p_forward(row, half):
         return remote(pwall.at[half, row], pwall.at[half, row], pf_send.at[row], pf_recv.at[row], sibling, sq)
 
-    def a_copy(step, head):
+    def a_copy(h, step, head):
         to = (sq + step) % N_SEQ
-        return remote(attsend.at[to], attin.at[head], a_send.at[step], a_recv.at[step], me, to)
+        return remote(attsend.at[h, to], attin.at[h, head], a_send.at[h, step], a_recv.at[h, step], me, to)
 
     def each(first, last, action):
         lax.fori_loop(first, last, lambda i, c: (action(i), c)[1], 0)
@@ -328,8 +328,8 @@
                 vc[clip, col * 2 + pair] = jnp.concatenate([values[:, cut] * inside, ones], axis=0).astype(BF16)
         return carry
 
+    on_core(1, hand_over)
     lax.fori_loop(0, NX, to_clips, 0)
-    on_core(1, hand_over)
 
     factor = math.log2(math.e) / math.sqrt(HD)
 
@@ -346,19 +346,23 @@
             att[clip, 2 * block + 1] = attended[:, 128:256]
         return carry
 
-    lax.fori_loop(0, CLIPS, attend, 0)
-
-    come = iota((512, 512), 0)
-    go = iota((512, 512), 1)
-    swap = jnp.where(come == ((go >> 6) & 3) * 128 + (go >> 8) * 64 + (go & 63), 1.0, 0.0).astype(BF16)
-    for pair in range(8):
-        blocks = jnp.concatenate([att[clip, pair] for clip in range(CLIPS)], axis=1)
-        swapped = mm(blocks, swap).astype(BF16)
-        for half in range(2):
-            attsend[((pair % 2) * 2 + half) * 4 + pair // 2] = swapped[:, half * ROWS:(half + 1) * ROWS]
-    each(1, N_SEQ, lambda i: a_copy(i, sq).start())
-    self_att = pltpu.make_async_copy(attsend.at[sq], attin.at[sq], local.at[5])
-    self_att.start()
+
+    come = iota((256, 256), 0)
+    go = iota((256, 256), 1)
+    swap = jnp.where(come == ((go >> 6) & 1) * 128 + (go >> 7) * 64 + (go & 63), 1.0, 0.0).astype(BF16)
+
+    def self_att(h):
+        return pltpu.make_async_copy(attsend.at[h, sq], attin.at[h, sq], local.at[2 + h])
+
+    for h in range(2):
+        lax.fori_loop(2 * h, 2 * h + 2, attend, 0)
+        for pair in range(8):
+            blocks = jnp.concatenate([att[2 * h, pair], att[2 * h + 1, pair]], axis=1)
+            swapped = mm(blocks, swap).astype(BF16)
+            for half in range(2):
+                attsend[h, ((pair % 2) * 2 + half) * 4 + pair // 2] = swapped[:, half * 128:(half + 1) * 128]
+        each(1, N_SEQ, lambda i: a_copy(h, i, sq).start())
+        self_att(h).start()
 
     each(0, 4, lambda i: p_forward(i, 1 - core).wait_recv())
     for pair in range(N_SEQ // 2):
@@ -369,9 +373,10 @@
         pwcat[rows, 0:HALF] = left.astype(BF16)
         pwcat[rows, HALF:D] = right[:, HALF - REST:].astype(BF16)
 
-    self_att.wait()
-    each(1, N_SEQ, lambda i: a_copy(i, (sq - i + N_SEQ) % N_SEQ).wait_recv())
-    heads = attin[...].astype(F32).reshape(N_SEQ * HD, ROWS).astype(BF16)
+    for h in range(2):
+        self_att(h).wait()
+        each(1, N_SEQ, lambda i: a_copy(h, i, (sq - i + N_SEQ) % N_SEQ).wait_recv())
+    heads = jnp.concatenate([attin[h].astype(F32).reshape(N_SEQ * HD, 128) for h in range(2)], axis=1).astype(BF16)
     for part in range(2):
         half_rows = ROWS // 2
         cut = slice(part * half_rows, (part + 1) * half_rows)
@@ -406,7 +411,8 @@
     to_sibling.wait_send()
     each(17, N_DP, lambda i: tok_out(i).wait_send())
     each(0, 4, lambda i: p_forward(i, core).wait_send())
-    each(1, N_SEQ, lambda i: a_copy(i, sq).wait_send())
+    for h in range(2):
+        each(1, N_SEQ, lambda i: a_copy(h, i, sq).wait_send())
 
     self_back.wait()
     ret_in((1 - core) * 16).wait_recv()
@@ -442,8 +448,8 @@
             pltpu.VMEM((CLIPS, 8, 128, HD), BF16),
             pltpu.VMEM((CLIPS, 8, HD + 8, 128), BF16),
             pltpu.VMEM((CLIPS, 8, HD, 128), BF16),
-            pltpu.VMEM((N_SEQ, HD, ROWS), BF16),
-            pltpu.VMEM((N_SEQ, HD, ROWS), BF16),
+            pltpu.VMEM((2, N_SEQ, HD, 128), BF16),
+            pltpu.VMEM((2, N_SEQ, HD, 128), BF16),
             pltpu.VMEM((N_DP, 8, D), BF16),
             pltpu.VMEM((N_DP, 8, D), BF16),
             pltpu.VMEM((512, 512), BF16),
@@ -454,7 +460,7 @@
             dma((N_DP,)), dma((N_DP,)),
             dma((CHUNKS, 4)), dma((CHUNKS, 4)), dma((CHUNKS, 4)), dma((CHUNKS, 4)),
             dma((4,)), dma((4,)), dma((4,)), dma((4,)),
-            dma((2, 4)), dma((2, 4)), dma((4,)), dma((4,)), dma((N_SEQ,)), dma((N_SEQ,)),
+            dma((2, 4)), dma((2, 4)), dma((4,)), dma((4,)), dma((2, N_SEQ)), dma((2, N_SEQ)),
             dma((N_DP,)), dma((N_DP,)),
             dma((8,)), dma((CHUNKS,)),
         ],

time: 110 us -> 109 us (level)
  no operation moved by 1% of the time
where the time goes in v4:
time: 109 us
  Pallas kernels  106 us (97%)
  local copies, waits for them, and re-layouts  2.5 us (2%)
    pallas_call x1, Pallas kernels, body(): pl.pallas_call(kernel, out_shape=jax.ShapeDtypeStruct((ROWS, D), BF16), i...  106 us

profile of v4, /device:TPU:1, one launch (start us, length us, event | category | flops | bytes accessed | tf_op | source)
XLA Modules:
  0.0 109.1 jit_solution(15016136718908855164)
XLA Ops:
  0.0 0.0 copy-start
  0.0 0.0 copy-start.1
  0.0 0.0 copy-start.2
  0.0 0.0 copy-start.3
  0.0 0.0 copy-start.4
  0.0 0.0 copy-start.5
  0.0 0.0 copy-start.6
  0.0 1.5 %reshape_squeeze.3.tok = bf16[256,1152]{1,0:T(8,128)(2,1)S(1)} reshape(bf16[1,64,4,1152]{3,2,1,0:T(4,128)(2,1)} %param.8) | data formatting | bytes 1179648 | tf_op jit(solution)/shard_map/reshape;squeeze | solution.py:473
  1.6 0.0 copy-done
  1.6 0.0 copy-done.1
  1.6 0.0 copy-done.2
  1.6 0.0 copy-done.3
  1.6 0.0 copy-done.4
  1.6 0.0 copy-done.5
  1.6 0.0 copy-done.6
  1.6 106.5 %block.1 = bf16[256,1152]{1,0:T(8,128)(2,1)S(1)} custom-call(bf16[256,1152]{1,0:T(8,128)(2,1)S(1)} %reshape_squeeze.3.tok, s32[1,64]{1,0:T(1,128)S(1)} %copy-done.5, s32[4,16]{1,0:T(4,128)S(1)} %bitcast.7, s32[1,4]{1,0:T(1,128)S(1)} %copy-done.6, bf16[3,4,1152]{2,1,0:T(4,128)(2,1)S(1)} %bitcast.6, bf16[3,72,1152]{2,1,0:T(8,128)(2,1)S(1)} %bitcast.5, ...), custom_call_target="tpu_custom_call" | custom-call | flops 5000000000 | bytes 4000000 | tf_op jit(solution)/shard_map/block/pallas_call | solution.py:431
  108.1 1.0 reshape.3
Async XLA Ops:
  0.0 1.6 %copy-start = (bf16[1152,3,72]{0,2,1:T(8,128)(2,1)S(1)}, bf16[1152,3,72]{0,2,1:T(8,128)(2,1)}, u32[]{:S(2)}) copy-start(bf16[1152,3,72]{0,2,1:T(8,128)(2,1)} %param.13) | copy-start | bytes 1492996
  0.0 1.6 %copy-start.1 = (bf16[72,1152]{1,0:T(8,128)(2,1)S(1)}, bf16[72,1152]{1,0:T(8,128)(2,1)}, u32[]{:S(2)}) copy-start(bf16[72,1152]{1,0:T(8,128)(2,1)} %pw.1) | copy-start | bytes 497668
  0.0 1.6 %copy-start.2 = (bf16[1,4,3,1152]{3,1,2,0:T(4,128)(2,1)S(1)}, bf16[1,4,3,1152]{3,1,2,0:T(4,128)(2,1)}, u32[]{:S(2)}) copy-start(bf16[1,4,3,1152]{3,1,2,0:T(4,128)(2,1)} %param.12) | copy-start | bytes 82948
  0.0 1.6 %copy-start.3 = (s32[1,4,16]{2,1,0:T(4,128)S(1)}, s32[1,4,16]{2,1,0:T(4,128)}, u32[]{:S(2)}) copy-start(s32[1,4,16]{2,1,0:T(4,128)} %param.10) | copy-start | bytes 772
  0.0 1.6 %copy-start.4 = (f32[2,72]{1,0:T(2,128)S(1)}, f32[2,72]{1,0:T(2,128)}, u32[]{:S(2)}) copy-start(f32[2,72]{1,0:T(2,128)} %gain.1) | copy-start | bytes 1732
  0.0 1.6 %copy-start.5 = (s32[1,64]{1,0:T(1,128)S(1)}, s32[1,64]{1,0:T(1,128)}, u32[]{:S(2)}) copy-start(s32[1,64]{1,0:T(1,128)} %owner.1) | copy-start | bytes 772
  0.0 1.6 %copy-start.6 = (s32[1,4]{1,0:T(1,128)S(1)}, s32[1,4]{1,0:T(1,128)}, u32[]{:S(2)}) copy-start(s32[1,4]{1,0:T(1,128)} %length.1) | copy-start | bytes 52

commit v5 on v4

--- a/solution.py
+++ b/solution.py
@@ -377,9 +377,9 @@
         self_att(h).wait()
         each(1, N_SEQ, lambda i: a_copy(h, i, (sq - i + N_SEQ) % N_SEQ).wait_recv())
     heads = jnp.concatenate([attin[h].astype(F32).reshape(N_SEQ * HD, 128) for h in range(2)], axis=1).astype(BF16)
-    for part in range(2):
-        half_rows = ROWS // 2
-        cut = slice(part * half_rows, (part + 1) * half_rows)
+    for part in range(4):
+        part_rows = ROWS // 4
+        cut = slice(part * part_rows, (part + 1) * part_rows)
         joined = mm_nt(unroute[cut, :], heads).astype(BF16)
         branch = mm(joined, pwcat[...])
         where = clip_col[cut, 0:1]
@@ -387,10 +387,10 @@
         position = ((where >> 2) & 15) * 64 + sq * 4 + (where & 3)
         limit = jnp.where(clip == 0, length[0, 0], jnp.where(
             clip == 1, length[0, 1], jnp.where(clip == 2, length[0, 2], length[0, 3])))
-        rows = arrived[part * 16:(part + 1) * 16].astype(F32).reshape(half_rows, D)
+        rows = arrived[part * 8:(part + 1) * 8].astype(F32).reshape(part_rows, D)
         result = jnp.where(position < limit, rows + of_its_clip(clip, 2) * branch, 0.0)
-        ret[part * 16:(part + 1) * 16] = result.reshape(16, 8, D).astype(BF16)
-        each(part * 16 + 2 * (1 - part), part * 16 + 16, lambda i: ret_out(i).start())
+        ret[part * 8:(part + 1) * 8] = result.reshape(8, 8, D).astype(BF16)
+        each(part * 8 + (2 if part == 0 else 0), part * 8 + 8, lambda i: ret_out(i).start())
     ret_out(1 - core).start()
     self_back = pltpu.make_async_copy(ret.at[core], back.at[core * 16], local.at[6])
     self_back.start()

time: 109 us -> 110 us (level)
  no operation moved by 1% of the time
where the time goes in v5:
time: 110 us; the launch traced here: 109 us
  Pallas kernels  107 us (97%)
  local copies, waits for them, and re-layouts  2.5 us (2%)
    pallas_call x1, Pallas kernels, body(): pl.pallas_call(kernel, out_shape=jax.ShapeDtypeStruct((ROWS, D), BF16), i...  107 us

profile of v5, /device:TPU:1, one launch (start us, length us, event | category | flops | bytes accessed | tf_op | source)
XLA Modules:
  0.0 109.4 jit_solution(2799704853350799472)
XLA Ops:
  0.0 0.0 copy-start
  0.0 0.0 copy-start.1
  0.0 0.0 copy-start.2
  0.0 0.0 copy-start.3
  0.0 0.0 copy-start.4
  0.0 0.0 copy-start.5
  0.0 0.0 copy-start.6
  0.0 1.5 %reshape_squeeze.3.tok = bf16[256,1152]{1,0:T(8,128)(2,1)S(1)} reshape(bf16[1,64,4,1152]{3,2,1,0:T(4,128)(2,1)} %param.8) | data formatting | bytes 1179648 | tf_op jit(solution)/shard_map/reshape;squeeze | solution.py:473
  1.6 0.0 copy-done
  1.6 0.0 copy-done.1
  1.6 0.0 copy-done.2
  1.6 0.0 copy-done.3
  1.6 0.0 copy-done.4
  1.6 0.0 copy-done.5
  1.6 0.0 copy-done.6
  1.6 106.8 %block.1 = bf16[256,1152]{1,0:T(8,128)(2,1)S(1)} custom-call(bf16[256,1152]{1,0:T(8,128)(2,1)S(1)} %reshape_squeeze.3.tok, s32[1,64]{1,0:T(1,128)S(1)} %copy-done.5, s32[4,16]{1,0:T(4,128)S(1)} %bitcast.7, s32[1,4]{1,0:T(1,128)S(1)} %copy-done.6, bf16[3,4,1152]{2,1,0:T(4,128)(2,1)S(1)} %bitcast.6, bf16[3,72,1152]{2,1,0:T(8,128)(2,1)S(1)} %bitcast.5, ...), custom_call_target="tpu_custom_call" | custom-call | flops 5000000000 | bytes 4000000 | tf_op jit(solution)/shard_map/block/pallas_call | solution.py:431
  108.5 1.0 reshape.3
Async XLA Ops:
  0.0 1.6 %copy-start = (bf16[1152,3,72]{0,2,1:T(8,128)(2,1)S(1)}, bf16[1152,3,72]{0,2,1:T(8,128)(2,1)}, u32[]{:S(2)}) copy-start(bf16[1152,3,72]{0,2,1:T(8,128)(2,1)} %param.13) | copy-start | bytes 1492996
  0.0 1.6 %copy-start.1 = (bf16[72,1152]{1,0:T(8,128)(2,1)S(1)}, bf16[72,1152]{1,0:T(8,128)(2,1)}, u32[]{:S(2)}) copy-start(bf16[72,1152]{1,0:T(8,128)(2,1)} %pw.1) | copy-start | bytes 497668
  0.0 1.6 %copy-start.2 = (bf16[1,4,3,1152]{3,1,2,0:T(4,128)(2,1)S(1)}, bf16[1,4,3,1152]{3,1,2,0:T(4,128)(2,1)}, u32[]{:S(2)}) copy-start(bf16[1,4,3,1152]{3,1,2,0:T(4,128)(2,1)} %param.12) | copy-start | bytes 82948
  0.0 1.6 %copy-start.3 = (s32[1,4,16]{2,1,0:T(4,128)S(1)}, s32[1,4,16]{2,1,0:T(4,128)}, u32[]{:S(2)}) copy-start(s32[1,4,16]{2,1,0:T(4,128)} %param.10) | copy-start | bytes 772
  0.0 1.6 %copy-start.4 = (f32[2,72]{1,0:T(2,128)S(1)}, f32[2,72]{1,0:T(2,128)}, u32[]{:S(2)}) copy-start(f32[2,72]{1,0:T(2,128)} %gain.1) | copy-start | bytes 1732
  0.0 1.6 %copy-start.5 = (s32[1,64]{1,0:T(1,128)S(1)}, s32[1,64]{1,0:T(1,128)}, u32[]{:S(2)}) copy-start(s32[1,64]{1,0:T(1,128)} %owner.1) | copy-start | bytes 772
  0.0 1.6 %copy-start.6 = (s32[1,4]{1,0:T(1,128)S(1)}, s32[1,4]{1,0:T(1,128)}, u32[]{:S(2)}) copy-start(s32[1,4]{1,0:T(1,128)} %length.1) | copy-start | bytes 52
